TPU v7x, 128 devices: a whole 4x4x4 slice. The times are simulated.
128 devices in a mesh: comp: 2 (over core), tile: 64 (over x, y, z).
Axes of the slice: x: 4, y: 4, z: 4, core: 2. Of those that a mesh axis runs over, the one named last changes fastest.
Arguments:
- state_field: float32 [2, 8, 24, 16, 8192], P('comp', None, None, None, 'tile'), may hold values from -6 to 6
- courant: float32 [2, 2, 8, 16, 8192], P('comp', None, None, None, 'tile'), may hold values from -0.3 to 0.3
- diffusivity: float32 [2, 8, 16, 8192], P('comp', None, None, 'tile'), may hold values from 0.1 to 10
- coupling_rate: float32 [2, 16, 8192], P('comp', None, 'tile'), may hold values from 0.2 to 1
- weight_table: bfloat16 [32, 128, 128], replicated, may hold values from -0.5 to 0.5
- source_row: int32 [2, 64, 384], P('comp', 'tile'), may hold values from 0 to 15
- destination_tile_ids: int32 [2, 64, 384, 1], P('comp', 'tile'), may hold values from 0 to 63; in each aligned block of 384 rows (0 to 383, 384 to 767, ..., all dimensions but the last counted through in order) at most 8 rows name the same one
- dest_row: int32 [2, 64, 384], P('comp', 'tile'), may hold values from 0 to 15
- weight_slot: int32 [2, 64, 384], P('comp', 'tile'), may hold values from 0 to 31
Outputs:
- new_state: float32 [2, 8, 24, 16, 8192], P('comp', None, None, None, 'tile')
Inputs may be any that keep to these rules, and one draw needn't show every extreme that they name: `destination_tile_ids`: among the 384 entries of one device no destination tile is named more than 8 times, and that bound is reached.
All inputs are finite; a program needn't handle non-finite values.
Results may differ from a plain program's by a relative error of at most 0.0037.
Values may be sent and summed in bfloat16 or wider, within the bound.
A program may use at most 128 MiB of HBM per device.

v0:
```python
import functools

import jax
import jax.numpy as jnp
from jax import lax
from jax.experimental import pallas as pl
from jax.experimental.pallas import tpu as pltpu
from jax.sharding import PartitionSpec as P

MESH = pl.DeviceIdType.MESH
NT = (((1,), (1,)), ((), ()))
STEPS = 4
LEV, FIELDS, CY, CX = 8, 24, 16, 128
ENTRIES, WTAB = 384, 32
GROUPS = 3
GF = FIELDS // GROUPS
SLABS = GF + 1
STRIDE = (16, 4, 1)
AXES = ((0, 1, 2), (1, 2, 0), (2, 0, 1))
F32, BF16, I32 = jnp.float32, jnp.bfloat16, jnp.int32


def iota(shape, dim):
    return lax.broadcasted_iota(I32, shape, dim)


def roll_lanes(value, shift):
    return pltpu.roll(value, shift % CX, 1)


def stencil_coefs(cx, cy):
    rows = iota(cx.shape, 0)
    cxp, cxm = jnp.maximum(cx, 0.0), jnp.minimum(cx, 0.0)
    cy = jnp.where(rows < CY - 1, cy, 0.0)
    cyp, cym = jnp.maximum(cy, 0.0), jnp.minimum(cy, 0.0)
    west = roll_lanes(cxp, 1)
    south = pltpu.roll(cyp, 1, 0)
    centre = 1.0 - cxp + roll_lanes(cxm, 1) - cyp + pltpu.roll(cym, 1, 0)
    return centre, -cxm, west, -cym, south


def advance(a, coefs):
    centre, east, west, north, south = coefs
    for step in range(STEPS):
        a = (
            centre * a
            + east * roll_lanes(a, CX - 1)
            + west * roll_lanes(a, 1)
            + north * pltpu.roll(a, CY - 1, 0)
            + south * pltpu.roll(a, 1, 0)
        )
    return a


def replicate(value):
    for shift in (16, 32, 64):
        value = value + roll_lanes(value, shift)
    return value


def kernel(
    state_hbm,
    courant_ref,
    diff_ref,
    rate_ref,
    weight_hbm,
    srow_ref,
    dest_ref,
    drow_ref,
    wslot_ref,
    solved_hbm,
    gain_ref,
    incoming_ref,
    state,
    weight,
    packed,
    cpacked,
    halo_out,
    halo_in,
    fixed,
    gath,
    pick,
    spread,
    outgoing,
    arrived,
    solve_coef,
    load_sem,
    weight_sem,
    store_sem,
    ag_send,
    ag_recv,
    halo_send,
    halo_recv,
    sc_send,
    sc_recv,
):
    comp, tile = lax.axis_index("comp"), lax.axis_index("tile")
    coords = (tile >> 4, (tile >> 2) & 3, tile & 3)

    def shifted(axis, step):
        return tile + (((coords[axis] + step) & 3) - coords[axis]) * STRIDE[axis]

    loads = [
        pltpu.make_async_copy(state_hbm.at[k], state.at[k], load_sem.at[k]) for k in range(LEV)
    ]
    for load in loads:
        load.start()
    weight_load = pltpu.make_async_copy(weight_hbm, weight, weight_sem)
    weight_load.start()

    right, left = (tile + 1) & 63, (tile + 63) & 63
    barrier = pltpu.get_barrier_semaphore()
    greeted = [(comp, shifted(axis, step)) for axis in range(3) for step in (1, 3)]
    greeted += [(comp, right), (comp, left), (1 - comp, tile)]
    greeted += [(1 - comp, shifted(axis, step)) for axis in range(3) for step in (1, 2, 3)]
    for target in greeted:
        pl.semaphore_signal(barrier, inc=1, device_id=target, device_id_type=MESH)

    targets = dest_ref[...]
    srow, drow, wslot = srow_ref[...], drow_ref[...], wslot_ref[...]
    named = (iota((64, ENTRIES), 0) == targets).astype(F32)
    before = (iota((ENTRIES, ENTRIES), 0) < iota((ENTRIES, ENTRIES), 1)).astype(F32)
    counts = jnp.dot(named.astype(BF16), before.astype(BF16), preferred_element_type=F32)
    rank = jnp.sum(named * counts, axis=0, keepdims=True).astype(I32)
    rel = (
        ((targets >> 4) - coords[0]) & 3,
        ((targets >> 2) - coords[1]) & 3,
        (targets - coords[2]) & 3,
    )
    kind, quarter = iota((16, ENTRIES), 0) >> 2, iota((16, ENTRIES), 0) & 3
    values = jnp.where(kind == 0, wslot, jnp.where(kind == 1, srow, drow + 1))
    for g, (u, v, q) in enumerate(AXES):
        spot = (rel[u] * 4 + rel[v]) * 8 + rank
        hot = (iota((CX, ENTRIES), 0) == spot).astype(F32).astype(BF16)
        kept = jnp.where((quarter == rel[q]) & (kind < 3), values, 0)
        table = lax.dot_general(kept.astype(F32).astype(BF16), hot, NT, preferred_element_type=F32)
        gath[g, 0, 0, GF] = table.astype(BF16)

    loads[0].wait()
    for g in range(GROUPS):
        gath[g, 0, 0, :GF] = state[0, g * GF : (g + 1) * GF].astype(BF16)

    pl.semaphore_wait(barrier, len(greeted))

    def remote(src, dst, send, recv, target):
        return pltpu.make_async_remote_copy(
            src_ref=src,
            dst_ref=dst,
            send_sem=send,
            recv_sem=recv,
            device_id=target,
            device_id_type=MESH,
        )

    def gather_copy(g, number):
        u, v, q = AXES[g]
        half = 5
        src, dst, axis, step = (
            (gath.at[g, 0, 0], gath.at[g, 0, 3], u, 1),
            (gath.at[g, 0, 0], gath.at[g, 0, 1], u, 3),
            (gath.at[g, 0, 3, pl.ds(0, half)], gath.at[g, 0, 2, pl.ds(0, half)], u, 1),
            (gath.at[g, 0, 1, pl.ds(half, SLABS - half)], gath.at[g, 0, 2, pl.ds(half, SLABS - half)], u, 3),
            (gath.at[g, 0], gath.at[g, 3], v, 1),
            (gath.at[g, 0], gath.at[g, 1], v, 3),
            (gath.at[g, 3, pl.ds(0, 2)], gath.at[g, 2, pl.ds(0, 2)], v, 1),
            (gath.at[g, 1, pl.ds(2, 2)], gath.at[g, 2, pl.ds(2, 2)], v, 3),
        )[number]
        return remote(src, dst, ag_send.at[g, number], ag_recv.at[g, number], (comp, shifted(axis, step)))

    gathers = [[gather_copy(g, number) for number in range(8)] for g in range(GROUPS)]

    def start_pair(phase):
        for g in range(GROUPS):
            gathers[g][2 * phase].start()
            gathers[g][2 * phase + 1].start()

    def wait_pair(phase):
        for g in range(GROUPS):
            gathers[g][2 * phase].wait_recv()
            gathers[g][2 * phase + 1].wait_recv()

    start_pair(0)

    for load in loads[1:]:
        load.wait()
    lanes = iota((CY, CX), 1)
    group_of, place = lanes >> 4, lanes & 15

    def pack_level(k, carry):
        for m in range(GROUPS):
            value = roll_lanes(state[k, m * 8], 8)
            for i in range(1, 8):
                value = jnp.where(group_of == i, roll_lanes(state[k, m * 8 + i], 16 * i + 8), value)
            packed[k * 3 + m] = value
        for c in range(2):
            cpacked[c, k] = replicate(jnp.where(lanes < 16, roll_lanes(courant_ref[c, k], 8), 0.0))
        return carry

    lax.fori_loop(0, LEV, pack_level, 0)
    quad = (lanes >> 2) & 3
    for n in range(6):
        for side, base in ((0, 4), (1, 8)):
            value = roll_lanes(packed[4 * n], -base)
            for t in range(1, 4):
                value = jnp.where(quad == t, roll_lanes(packed[4 * n + t], 4 * t - base), value)
            halo_out[side, n] = value
    for side, base in ((0, 4), (1, 8)):
        value = roll_lanes(cpacked[0, 0], -base)
        for e in range(1, 16):
            moved = roll_lanes(cpacked[e // 8, e % 8], 4 * (e % 4) - base)
            value = jnp.where((lanes >> 2) == e, moved, value)
        halo_out[side, 6] = value
    halos = [
        remote(halo_out.at[side], halo_in.at[side], halo_send.at[side], halo_recv.at[side], (comp, target))
        for side, target in ((0, right), (1, left))
    ]
    for copy in halos:
        copy.start()

    wait_pair(0)
    start_pair(1)

    def transport_level(k, carry):
        coefs = stencil_coefs(courant_ref[0, k], courant_ref[1, k])

        def fields(n, inner):
            for j in range(4):
                state[k, n * 4 + j] = advance(state[k, n * 4 + j], coefs)
            return inner

        return lax.fori_loop(0, FIELDS // 4, fields, carry)

    lax.fori_loop(0, 1, transport_level, 0)
    wait_pair(1)
    start_pair(2)
    lax.fori_loop(1, 6, transport_level, 0)
    wait_pair(2)
    start_pair(3)
    lax.fori_loop(6, LEV, transport_level, 0)

    ratio = jnp.zeros((CY, CX), F32)
    gain = None
    gains, ratios = [], []
    for k in range(LEV):
        above = diff_ref[k] if k < LEV - 1 else jnp.zeros((CY, CX), F32)
        below = diff_ref[k - 1] if k > 0 else jnp.zeros((CY, CX), F32)
        inverse = 1.0 / (1.0 + below + above - below * ratio)
        ratio = above * inverse
        solve_coef[0, k] = inverse
        solve_coef[1, k] = below * inverse
        solve_coef[2, k] = ratio
        gain = inverse if k == 0 else below * inverse * gain
        gains.append(gain)
        ratios.append(ratio)
    value = jnp.zeros((CY, CX), F32)
    for k in reversed(range(LEV)):
        value = gains[k] + ratios[k] * value
        gain_ref[k] = value * rate_ref[...]

    for copy in halos:
        copy.wait_recv()

    def strip_level(k, carry):
        cl, cr = [], []
        for c in range(2):
            e = c * 8 + k
            from_left = roll_lanes(halo_in[0, 6], CX - 4 * e)
            from_right = roll_lanes(halo_in[1, 6], CX - 4 * e)
            from_left = replicate(jnp.where(lanes < 4, from_left, 0.0))
            from_right = replicate(jnp.where(lanes < 4, from_right, 0.0))
            own = cpacked[c, k]
            cl.append(jnp.where(place < 4, from_left, roll_lanes(own, -4)))
            cr.append(jnp.where((place >= 8) & (place < 12), roll_lanes(from_right, 8), own))
        coefs_left, coefs_right = stencil_coefs(*cl), stencil_coefs(*cr)
        for m in range(3):
            p = k * 3 + m
            n, t = p >> 2, p & 3
            own = packed[p]
            a_left = jnp.where(place < 4, roll_lanes(halo_in[0, n], CX - 4 * t), roll_lanes(own, -4))
            a_right = jnp.where(
                (place >= 8) & (place < 12), roll_lanes(halo_in[1, n], CX + 8 - 4 * t), own
            )
            a_left, a_right = advance(a_left, coefs_left), advance(a_right, coefs_right)
            fixed[p] = jnp.where(place < 4, roll_lanes(a_right, -4), a_left)
        return carry

    lax.fori_loop(0, LEV, strip_level, 0)

    weight_load.wait()
    rows_p, rows_q = iota((WTAB * CY, CX), 0), iota((256, CX), 0)
    lane_p = iota((1, CX), 1) >> 3
    scatters = []
    for g, (u, v, q) in enumerate(AXES):
        for number in (6, 7):
            gathers[g][number].wait_recv()
        table = jnp.zeros((CY, CX), F32)
        for p in range(16):
            rv, ru = p // 4, p % 4
            offset = ((-ru % 4) * 4 + (-rv % 4)) * 8
            moved = roll_lanes(gath[g, rv, ru, GF].astype(F32), p * 8 - offset)
            table = jnp.where((lanes >> 3) == p, moved, table)
        codes = table.astype(I32)
        for d in range(4):
            w_e, r_e, y_e = codes[d : d + 1], codes[4 + d : 5 + d], codes[8 + d : 9 + d]
            into = (rows_p == jnp.where(y_e > 0, w_e * CY + y_e - 1, -1)).astype(F32).astype(BF16)
            outof = (rows_q == lane_p * CY + r_e).astype(F32).astype(BF16)
            pick[d] = lax.dot_general(into, outof, NT, preferred_element_type=F32).astype(BF16)

        def spread_quarter(d, carry):
            chosen = pick[d]
            for pair in range(GF // 2):
                blocks = jnp.concatenate(
                    [gath[g, :, :, 2 * pair + h].reshape(256, CX) for h in range(2)], axis=1
                )
                summed = jnp.dot(chosen, blocks, preferred_element_type=F32).astype(BF16)
                for h in range(2):
                    for w in range(WTAB):
                        spread[d, w, pl.ds((2 * pair + h) * CY, CY)] = summed[
                            w * CY : (w + 1) * CY, h * CX : (h + 1) * CX
                        ]
            return carry

        lax.fori_loop(0, 4, spread_quarter, 0)
        table_all = jnp.concatenate([weight[w] for w in range(WTAB)], axis=1)
        for d2 in range(2):
            chosen = jnp.concatenate(
                [
                    jnp.concatenate([spread[2 * d2, w], spread[2 * d2 + 1, w]], axis=0)
                    for w in range(WTAB)
                ],
                axis=1,
            )
            result = lax.dot_general(chosen, table_all, NT, preferred_element_type=F32).astype(BF16)
            for h in range(2):
                outgoing[g, 2 * d2 + h] = result[h * 128 : (h + 1) * 128].reshape(GF, CY, CX)
        for d in range(4):
            target = (1 - comp, tile if d == 0 else shifted(q, d))
            copy = remote(
                outgoing.at[g, d], arrived.at[g, (4 - d) % 4], sc_send.at[g, d], sc_recv.at[g, d], target
            )
            copy.start()
            scatters.append(copy)

    edge = (lanes < 4) | (lanes >= CX - 4)

    def solve_field(f, carry):
        m, turn = f >> 3, CX - 4 - 16 * (f & 7)
        solved = jnp.zeros((CY, CX), F32)
        kept = []
        for k in range(LEV):
            value = jnp.where(edge, roll_dynamic(fixed[k * 3 + m], turn), state[k, f])
            solved = solve_coef[0, k] * value + solve_coef[1, k] * solved
            kept.append(solved)
        upper = kept[-1]
        state[LEV - 1, f] = upper
        for k in reversed(range(LEV - 1)):
            upper = kept[k] + solve_coef[2, k] * upper
            state[k, f] = upper
        return carry

    lax.fori_loop(0, FIELDS, solve_field, 0)
    store = pltpu.make_async_copy(state, solved_hbm, store_sem)
    store.start()

    for copy in scatters:
        copy.wait_recv()
    for g in range(GROUPS):
        total = arrived[g, 0].astype(F32)
        for d in range(1, 4):
            total = total + arrived[g, d].astype(F32)
        incoming_ref[g * GF : (g + 1) * GF] = total

    for g in range(GROUPS):
        for copy in gathers[g]:
            copy.wait_send()
    for copy in halos:
        copy.wait_send()
    for copy in scatters:
        copy.wait_send()
    store.wait()


def roll_dynamic(value, shift):
    return pltpu.roll(value, shift, 1)


def per_device(
    state_field,
    courant,
    diffusivity,
    coupling_rate,
    weight_table,
    source_row,
    destination_tile_ids,
    dest_row,
    weight_slot,
):
    vmem, anywhere = pl.BlockSpec(memory_space=pltpu.VMEM), pl.BlockSpec(memory_space=pl.ANY)
    plane = (CY, CX)
    solved, gain, incoming = pl.pallas_call(
        kernel,
        out_shape=(
            jax.ShapeDtypeStruct((LEV, FIELDS) + plane, F32),
            jax.ShapeDtypeStruct((LEV,) + plane, F32),
            jax.ShapeDtypeStruct((FIELDS,) + plane, F32),
        ),
        in_specs=[anywhere, vmem, vmem, vmem, anywhere, vmem, vmem, vmem, vmem],
        out_specs=(anywhere, vmem, vmem),
        scratch_shapes=[
            pltpu.VMEM((LEV, FIELDS) + plane, F32),
            pltpu.VMEM((WTAB, CX, CX), BF16),
            pltpu.VMEM((24,) + plane, F32),
            pltpu.VMEM((2, LEV) + plane, F32),
            pltpu.VMEM((2, 7) + plane, F32),
            pltpu.VMEM((2, 7) + plane, F32),
            pltpu.VMEM((24,) + plane, F32),
            pltpu.VMEM((GROUPS, 4, 4, SLABS) + plane, BF16),
            pltpu.VMEM((4, WTAB * CY, 256), BF16),
            pltpu.VMEM((4, WTAB, GF * CY, CX), BF16),
            pltpu.VMEM((GROUPS, 4, GF) + plane, BF16),
            pltpu.VMEM((GROUPS, 4, GF) + plane, BF16),
            pltpu.VMEM((3, LEV) + plane, F32),
            pltpu.SemaphoreType.DMA((LEV,)),
            pltpu.SemaphoreType.DMA,
            pltpu.SemaphoreType.DMA,
            pltpu.SemaphoreType.DMA((GROUPS, 8)),
            pltpu.SemaphoreType.DMA((GROUPS, 8)),
            pltpu.SemaphoreType.DMA((2,)),
            pltpu.SemaphoreType.DMA((2,)),
            pltpu.SemaphoreType.DMA((GROUPS, 4)),
            pltpu.SemaphoreType.DMA((GROUPS, 4)),
        ],
        compiler_params=pltpu.CompilerParams(
            collective_id=0, has_side_effects=True, vmem_limit_bytes=48 * 2**20
        ),
        name="interval",
    )(
        state_field[0],
        courant[0],
        diffusivity[0],
        coupling_rate[0],
        weight_table,
        source_row[0],
        destination_tile_ids.reshape(1, ENTRIES),
        dest_row[0],
        weight_slot[0],
    )
    return (solved + gain[:, None] * incoming[None])[None]


def solution(mesh):
    return jax.shard_map(
        per_device,
        mesh=mesh,
        in_specs=(
            P("comp", None, None, None, "tile"),
            P("comp", None, None, None, "tile"),
            P("comp", None, None, "tile"),
            P("comp", None, "tile"),
            P(),
            P("comp", "tile", None),
            P("comp", "tile", None, None),
            P("comp", "tile", None),
            P("comp", "tile", None),
        ),
        out_specs=P("comp", None, None, None, "tile"),
        check_vma=False,
    )
```

profile of v0, /device:TPU:1, one launch (start us, length us, event | category | flops | bytes accessed | tf_op | source)
XLA Modules:
  0.0 63.7 jit_solution(1648564304352284803)
XLA Ops:
  0.0 0.0 copy-start
  0.0 1.4 %copy-done = f32[1,8,24,16,128]{4,3,2,1,0:T(8,128)S(1)} copy-done((f32[1,8,24,16,128]{4,3,2,1,0:T(8,128)S(1)}, f32[1,8,24,16,128]{4,3,2,1,0:T(8,128)}, u32[]{:S(2)}) %copy-start) | copy-done | bytes 1572888
  1.4 0.0 copy-start.1
  1.4 1.2 %copy-done.1 = bf16[32,128,128]{2,1,0:T(8,128)(2,1)S(1)} copy-done((bf16[32,128,128]{2,1,0:T(8,128)(2,1)S(1)}, bf16[32,128,128]{2,1,0:T(8,128)(2,1)}, u32[]{:S(2)}) %copy-start.1) | copy-done | bytes 1048600
  2.6 0.0 copy-start.2
  2.6 0.9 %copy-done.2 = f32[1,2,8,16,128]{4,3,2,1,0:T(8,128)S(1)} copy-done((f32[1,2,8,16,128]{4,3,2,1,0:T(8,128)S(1)}, f32[1,2,8,16,128]{4,3,2,1,0:T(8,128)}, u32[]{:S(2)}) %copy-start.2) | copy-done | bytes 131096
  3.5 0.0 copy-start.3
  3.5 0.8 %copy-done.3 = f32[1,8,16,128]{3,2,1,0:T(8,128)S(1)} copy-done((f32[1,8,16,128]{3,2,1,0:T(8,128)S(1)}, f32[1,8,16,128]{3,2,1,0:T(8,128)}, u32[]{:S(2)}) %copy-start.3) | copy-done | bytes 65560
  4.4 0.0 copy-start.4
  4.4 0.7 %copy-done.4 = f32[1,16,128]{2,1,0:T(8,128)S(1)} copy-done((f32[1,16,128]{2,1,0:T(8,128)S(1)}, f32[1,16,128]{2,1,0:T(8,128)}, u32[]{:S(2)}) %copy-start.4) | copy-done | bytes 8216
  5.1 0.0 copy-start.5
  5.1 0.7 %copy-done.5 = s32[1,1,384]{2,1,0:T(1,128)S(1)} copy-done((s32[1,1,384]{2,1,0:T(1,128)S(1)}, s32[1,1,384]{2,1,0:T(1,128)}, u32[]{:S(2)}) %copy-start.5) | copy-done | bytes 1560
  5.8 0.0 copy-start.6
  5.8 0.7 %copy-done.6 = s32[1,1,384,1]{2,3,1,0:T(1,128)S(1)} copy-done((s32[1,1,384,1]{2,3,1,0:T(1,128)S(1)}, s32[1,1,384,1]{2,3,1,0:T(1,128)}, u32[]{:S(2)}) %copy-start.6) | copy-done | bytes 1560
  6.4 0.0 copy-start.7
  6.4 0.7 %copy-done.7 = s32[1,1,384]{2,1,0:T(1,128)S(1)} copy-done((s32[1,1,384]{2,1,0:T(1,128)S(1)}, s32[1,1,384]{2,1,0:T(1,128)}, u32[]{:S(2)}) %copy-start.7) | copy-done | bytes 1560
  7.1 0.0 copy-start.8
  7.1 0.7 %copy-done.8 = s32[1,1,384]{2,1,0:T(1,128)S(1)} copy-done((s32[1,1,384]{2,1,0:T(1,128)S(1)}, s32[1,1,384]{2,1,0:T(1,128)}, u32[]{:S(2)}) %copy-start.8) | copy-done | bytes 1560
  7.8 54.6 %interval.1 = (f32[8,24,16,128]{3,2,1,0:T(8,128)S(1)}, f32[8,16,128]{2,1,0:T(8,128)S(1)}, f32[24,16,128]{2,1,0:T(8,128)S(1)}) custom-call(f32[8,24,16,128]{3,2,1,0:T(8,128)S(1)} %bitcast.10, f32[2,8,16,128]{3,2,1,0:T(8,128)S(1)} %bitcast.11, f32[8,16,128]{2,1,0:T(8,128)S(1)} %bitcast.12, f32[16,128]{1,0:T(8,128)S(1)} %bitcast.13, ...), custom_call_target="tpu_custom_call" | custom-call | tf_op jit(solution)/shard_map/interval/pallas_call | solution.py:400
  62.4 1.3 %add_bitcast_fusion = f32[1,8,24,16,128]{4,3,2,1,0:T(8,128)} fusion(f32[8,24,16,128]{3,2,1,0:T(8,128)S(1)} %get-tuple-element.8, f32[24,16,128]{2,1,0:T(8,128)S(1)} %get-tuple-element.10, f32[8,16,128]{2,1,0:T(8,128)S(1)} %get-tuple-element.9), kind=kLoop, calls=%fused_computation | loop fusion | flops 786432 | bytes 3407872 | tf_op jit(solution)/shard_map/broadcast_in_dim | solution.py:448
Async XLA Ops:
  0.0 1.4 %copy-start = (f32[1,8,24,16,128]{4,3,2,1,0:T(8,128)S(1)}, f32[1,8,24,16,128]{4,3,2,1,0:T(8,128)}, u32[]{:S(2)}) copy-start(f32[1,8,24,16,128]{4,3,2,1,0:T(8,128)} %param.9) | copy-start | bytes 4718596
  1.4 1.2 %copy-start.1 = (bf16[32,128,128]{2,1,0:T(8,128)(2,1)S(1)}, bf16[32,128,128]{2,1,0:T(8,128)(2,1)}, u32[]{:S(2)}) copy-start(bf16[32,128,128]{2,1,0:T(8,128)(2,1)} %weight_hbm.1) | copy-start | bytes 3145732
  2.6 0.9 %copy-start.2 = (f32[1,2,8,16,128]{4,3,2,1,0:T(8,128)S(1)}, f32[1,2,8,16,128]{4,3,2,1,0:T(8,128)}, u32[]{:S(2)}) copy-start(f32[1,2,8,16,128]{4,3,2,1,0:T(8,128)} %param.10) | copy-start | bytes 393220
  3.5 0.8 %copy-start.3 = (f32[1,8,16,128]{3,2,1,0:T(8,128)S(1)}, f32[1,8,16,128]{3,2,1,0:T(8,128)}, u32[]{:S(2)}) copy-start(f32[1,8,16,128]{3,2,1,0:T(8,128)} %param.11) | copy-start | bytes 196612
  4.4 0.7 %copy-start.4 = (f32[1,16,128]{2,1,0:T(8,128)S(1)}, f32[1,16,128]{2,1,0:T(8,128)}, u32[]{:S(2)}) copy-start(f32[1,16,128]{2,1,0:T(8,128)} %param.12) | copy-start | bytes 24580
  5.1 0.7 %copy-start.5 = (s32[1,1,384]{2,1,0:T(1,128)S(1)}, s32[1,1,384]{2,1,0:T(1,128)}, u32[]{:S(2)}) copy-start(s32[1,1,384]{2,1,0:T(1,128)} %param.14) | copy-start | bytes 4612
  5.8 0.7 %copy-start.6 = (s32[1,1,384,1]{2,3,1,0:T(1,128)S(1)}, s32[1,1,384,1]{2,3,1,0:T(1,128)}, u32[]{:S(2)}) copy-start(s32[1,1,384,1]{2,3,1,0:T(1,128)} %param.15) | copy-start | bytes 4612
  6.4 0.7 %copy-start.7 = (s32[1,1,384]{2,1,0:T(1,128)S(1)}, s32[1,1,384]{2,1,0:T(1,128)}, u32[]{:S(2)}) copy-start(s32[1,1,384]{2,1,0:T(1,128)} %param.16) | copy-start | bytes 4612
  7.1 0.7 %copy-start.8 = (s32[1,1,384]{2,1,0:T(1,128)S(1)}, s32[1,1,384]{2,1,0:T(1,128)}, u32[]{:S(2)}) copy-start(s32[1,1,384]{2,1,0:T(1,128)} %param.17) | copy-start | bytes 4612
where the time goes:
time: 64.1 us; the launch traced here: 63.7 us
  Pallas kernels  54.6 us (85%)
  local copies, waits for them, and re-layouts  7.79 us (12%)
  other arithmetic  1.3 us (2%)
    pallas_call x1, Pallas kernels, per_device(): pl.pallas_call(kernel, out_shape=(jax.ShapeDtypeStruct((LEV, FIELDS) + pl...  54.6 us
    unnamed x18, local copies, waits for them, and re-layouts  7.79 us
    broadcast_in_dim x1, other arithmetic, per_device(): return (solved + gain[:, None] * incoming[None])[None]  1.3 us

commit v1 on v0

v1 whole, which is shorter than its diff:
```python
import jax
import jax.numpy as jnp
from jax import lax
from jax.experimental import pallas as pl
from jax.experimental.pallas import tpu as pltpu
from jax.sharding import PartitionSpec as P

MESH = pl.DeviceIdType.MESH
NT = (((1,), (1,)), ((), ()))
ORDER = (0, 1, 3, 2)
LEV, FIELDS, CY, CX = 8, 24, 16, 128
ENTRIES, WTAB = 384, 32
GROUPS = 3
GF = FIELDS // GROUPS
SLABS = GF + 1
STRIDE = (16, 4, 1)
AXES = ((0, 1, 2), (1, 2, 0), (2, 0, 1))
F32, BF16, I32 = jnp.float32, jnp.bfloat16, jnp.int32


def iota(shape, dim):
    return lax.broadcasted_iota(I32, shape, dim)


def roll_lanes(value, shift):
    return pltpu.roll(value, shift % CX, 1)


def stencil_coefs(cx, cy):
    rows = iota(cx.shape, 0)
    cxp, cxm = jnp.maximum(cx, 0.0), jnp.minimum(cx, 0.0)
    cy = jnp.where(rows < CY - 1, cy, 0.0)
    cyp, cym = jnp.maximum(cy, 0.0), jnp.minimum(cy, 0.0)
    west = roll_lanes(cxp, 1)
    south = pltpu.roll(cyp, 1, 0)
    centre = 1.0 - cxp + roll_lanes(cxm, 1) - cyp + pltpu.roll(cym, 1, 0)
    return centre, -cxm, west, -cym, south


def one_step(a, coefs):
    centre, east, west, north, south = coefs
    return (
        centre * a
        + east * roll_lanes(a, CX - 1)
        + west * roll_lanes(a, 1)
        + north * pltpu.roll(a, CY - 1, 0)
        + south * pltpu.roll(a, 1, 0)
    )


def replicate(value):
    for shift in (16, 32, 64):
        value = value + roll_lanes(value, shift)
    return value


def kernel(
    state_hbm,
    courant_hbm,
    diff_hbm,
    rate_hbm,
    weight_hbm,
    srow_hbm,
    dest_hbm,
    drow_hbm,
    wslot_hbm,
    solved_hbm,
    gain_ref,
    incoming_ref,
    state,
    courant_ref,
    diff_ref,
    rate_ref,
    entries,
    weight,
    packed,
    cpacked,
    strips,
    strip_coef,
    halo_out,
    halo_in,
    coef,
    gath,
    pick,
    spread,
    outgoing,
    arrived,
    solve_coef,
    load_sem,
    entry_sem,
    small_sem,
    store_sem,
    ag_send,
    ag_recv,
    halo_send,
    halo_recv,
    sc_send,
    sc_recv,
):
    comp, tile = lax.axis_index("comp"), lax.axis_index("tile")
    coords = (tile >> 4, (tile >> 2) & 3, tile & 3)

    def shifted(axis, step):
        return tile + (((coords[axis] + step) & 3) - coords[axis]) * STRIDE[axis]

    right, left = (tile + 1) & 63, (tile + 63) & 63
    barrier = pltpu.get_barrier_semaphore()
    greeted = [(comp, shifted(axis, step)) for axis in range(3) for step in (1, 3)]
    greeted += [(comp, right), (comp, left), (1 - comp, tile)]
    greeted += [(1 - comp, shifted(axis, step)) for axis in range(3) for step in (1, 2, 3)]
    for target in greeted:
        pl.semaphore_signal(barrier, inc=1, device_id=target, device_id_type=MESH)

    loads = [
        pltpu.make_async_copy(state_hbm.at[k], state.at[k], load_sem.at[k]) for k in range(LEV)
    ]
    entry_loads = [
        pltpu.make_async_copy(source, entries.at[pl.ds(n, 1)], entry_sem.at[n])
        for n, source in enumerate((dest_hbm, srow_hbm, drow_hbm, wslot_hbm))
    ]
    small_loads = [
        pltpu.make_async_copy(source, target, small_sem.at[n])
        for n, (source, target) in enumerate(
            ((courant_hbm, courant_ref), (diff_hbm, diff_ref), (rate_hbm, rate_ref), (weight_hbm, weight))
        )
    ]
    loads[0].start()
    for load in entry_loads:
        load.start()
    small_loads[0].start()
    for load in loads[1:]:
        load.start()
    for load in small_loads[1:]:
        load.start()

    for load in entry_loads:
        load.wait()
    targets, srow, drow, wslot = (entries[n : n + 1] for n in range(4))
    named = (iota((64, ENTRIES), 0) == targets).astype(F32)
    before = (iota((ENTRIES, ENTRIES), 0) < iota((ENTRIES, ENTRIES), 1)).astype(F32)
    counts = jnp.dot(named.astype(BF16), before.astype(BF16), preferred_element_type=F32)
    rank = jnp.sum(named * counts, axis=0, keepdims=True).astype(I32)
    rel = (
        ((targets >> 4) - coords[0]) & 3,
        ((targets >> 2) - coords[1]) & 3,
        (targets - coords[2]) & 3,
    )
    kind, quarter = iota((16, ENTRIES), 0) >> 2, iota((16, ENTRIES), 0) & 3
    values = jnp.where(kind == 0, wslot, jnp.where(kind == 1, srow, drow + 1))
    for g, (u, v, q) in enumerate(AXES):
        spot = (rel[u] * 4 + rel[v]) * 8 + rank
        hot = (iota((CX, ENTRIES), 0) == spot).astype(F32).astype(BF16)
        kept = jnp.where((quarter == rel[q]) & (kind < 3), values, 0)
        table = lax.dot_general(kept.astype(F32).astype(BF16), hot, NT, preferred_element_type=F32)
        gath[g, 0, 0, GF] = table.astype(BF16)

    loads[0].wait()
    for g in range(GROUPS):
        gath[g, 0, 0, :GF] = state[0, g * GF : (g + 1) * GF].astype(BF16)

    pl.semaphore_wait(barrier, len(greeted))

    def remote(src, dst, send, recv, target):
        return pltpu.make_async_remote_copy(
            src_ref=src,
            dst_ref=dst,
            send_sem=send,
            recv_sem=recv,
            device_id=target,
            device_id_type=MESH,
        )

    def gather_copy(g, number):
        u, v, q = AXES[g]
        block = lambda i, j: gath.at[g, i, j]
        low, high = pl.ds(0, 5), pl.ds(5, SLABS - 5)
        src, dst, axis, step = (
            (block(0, 0), block(0, 2), u, 1),
            (block(0, 0), block(0, 1), u, 3),
            (block(0, 0), block(2, 0), v, 1),
            (block(0, 0), block(1, 0), v, 3),
            (gath.at[g, 0, 2, low], gath.at[g, 0, 3, low], u, 1),
            (gath.at[g, 0, 1, high], gath.at[g, 0, 3, high], u, 3),
            (gath.at[g, 0, pl.ds(1, 2)], gath.at[g, 2, pl.ds(1, 2)], v, 1),
            (gath.at[g, 0, pl.ds(1, 2)], gath.at[g, 1, pl.ds(1, 2)], v, 3),
            (block(2, 0), block(3, 0), v, 1),
            (block(0, 3), block(2, 3), v, 1),
            (block(0, 3), block(1, 3), v, 3),
            (block(2, 1), block(3, 1), v, 1),
            (block(1, 2), block(3, 2), v, 3),
            (block(1, 3), block(3, 3), v, 3),
        )[number]
        return remote(src, dst, ag_send.at[g, number], ag_recv.at[g, number], (comp, shifted(axis, step)))

    gathers = [[gather_copy(g, number) for number in range(14)] for g in range(GROUPS)]
    rounds = ((0, 1, 2, 3), (4, 5, 6, 7, 8), (9, 10, 11, 12), (13,))

    def start_round(n):
        for number in rounds[n]:
            for g in range(GROUPS):
                gathers[g][number].start()

    def wait_round(n):
        for number in rounds[n]:
            for g in range(GROUPS):
                gathers[g][number].wait_recv()

    start_round(0)

    for load in loads[1:]:
        load.wait()
    small_loads[0].wait()
    lanes = iota((CY, CX), 1)
    group_of, place = lanes >> 4, lanes & 15

    def pack_level(k, carry):
        for m in range(3):
            value = roll_lanes(state[k, m * 8], 8)
            for i in range(1, 8):
                value = jnp.where(group_of == i, roll_lanes(state[k, m * 8 + i], 16 * i + 8), value)
            packed[k * 3 + m] = value
        return carry

    lax.fori_loop(0, LEV, pack_level, 0)
    planes = [(c, k) for c in range(2) for k in range(LEV)]
    for c, k in planes:
        cpacked[c, k] = replicate(jnp.where(lanes < 16, roll_lanes(courant_ref[c, k], 8), 0.0))
    quad = (lanes >> 2) & 3
    for n in range(6):
        for side, base in ((0, 4), (1, 8)):
            value = roll_lanes(packed[4 * n], -base)
            for t in range(1, 4):
                value = jnp.where(quad == t, roll_lanes(packed[4 * n + t], 4 * t - base), value)
            halo_out[side, n] = value
    for side, base in ((0, 4), (1, 8)):
        value = roll_lanes(cpacked[0, 0], -base)
        for e in range(1, 16):
            moved = roll_lanes(cpacked[e // 8, e % 8], 4 * (e % 4) - base)
            value = jnp.where((lanes >> 2) == e, moved, value)
        halo_out[side, 6] = value
    halos = [
        remote(halo_out.at[side], halo_in.at[side], halo_send.at[side], halo_recv.at[side], (comp, target))
        for side, target in ((0, right), (1, left))
    ]
    for copy in halos:
        copy.start()

    wait_round(0)
    start_round(1)

    def coef_level(k, carry):
        for n, value in enumerate(stencil_coefs(courant_ref[0, k], courant_ref[1, k])):
            coef[k, n] = value
        return carry

    for k in range(LEV):
        coef_level(k, 0)

    def transport_step(n, carry):
        k = n >> 2
        coefs = [coef[k, n] for n in range(5)]
        for f in range(FIELDS):
            state[k, f] = one_step(state[k, f], coefs)
        return carry

    lax.fori_loop(0, 4, transport_step, 0)
    wait_round(1)
    start_round(2)
    lax.fori_loop(4, 16, transport_step, 0)
    wait_round(2)
    start_round(3)
    lax.fori_loop(16, 32, transport_step, 0)

    small_loads[3].wait()
    wait_round(3)
    rows_p, rows_q = iota((WTAB * CY, CX), 0), iota((256, CX), 0)
    lane_p = iota((1, CX), 1) >> 3
    scatters = []
    for g, (u, v, q) in enumerate(AXES):
        table = jnp.zeros((CY, CX), F32)
        for p in range(16):
            rv, ru = ORDER[p // 4], ORDER[p % 4]
            offset = ((-ru % 4) * 4 + (-rv % 4)) * 8
            moved = roll_lanes(gath[g, p // 4, p % 4, GF].astype(F32), p * 8 - offset)
            table = jnp.where((lanes >> 3) == p, moved, table)
        codes = table.astype(I32)
        for d in range(4):
            w_e, r_e, y_e = codes[d : d + 1], codes[4 + d : 5 + d], codes[8 + d : 9 + d]
            into = (rows_p == jnp.where(y_e > 0, w_e * CY + y_e - 1, -1)).astype(F32).astype(BF16)
            outof = (rows_q == lane_p * CY + r_e).astype(F32).astype(BF16)
            pick[d] = lax.dot_general(into, outof, NT, preferred_element_type=F32).astype(BF16)

        def spread_quarter(d, carry):
            chosen = pick[d]
            for pair in range(GF // 2):
                blocks = jnp.concatenate(
                    [gath[g, :, :, 2 * pair + h].reshape(256, CX) for h in range(2)], axis=1
                )
                summed = jnp.dot(chosen, blocks, preferred_element_type=F32).astype(BF16)
                for h in range(2):
                    for w in range(WTAB):
                        spread[d, w, pl.ds((2 * pair + h) * CY, CY)] = summed[
                            w * CY : (w + 1) * CY, h * CX : (h + 1) * CX
                        ]
            return carry

        lax.fori_loop(0, 4, spread_quarter, 0)
        table_all = jnp.concatenate([weight[w] for w in range(WTAB)], axis=1)
        for d2 in range(2):
            chosen = jnp.concatenate(
                [
                    jnp.concatenate([spread[2 * d2, w], spread[2 * d2 + 1, w]], axis=0)
                    for w in range(WTAB)
                ],
                axis=1,
            )
            result = lax.dot_general(chosen, table_all, NT, preferred_element_type=F32).astype(BF16)
            for h in range(2):
                outgoing[g, 2 * d2 + h] = result[h * 128 : (h + 1) * 128].reshape(GF, CY, CX)
        for d in range(4):
            target = (1 - comp, tile if d == 0 else shifted(q, d))
            copy = remote(
                outgoing.at[g, d], arrived.at[g, (4 - d) % 4], sc_send.at[g, d], sc_recv.at[g, d], target
            )
            copy.start()
            scatters.append(copy)

    small_loads[1].wait()
    small_loads[2].wait()
    ratio = jnp.zeros((CY, CX), F32)
    gain = None
    gains, ratios = [], []
    for k in range(LEV):
        above = diff_ref[k] if k < LEV - 1 else jnp.zeros((CY, CX), F32)
        below = diff_ref[k - 1] if k > 0 else jnp.zeros((CY, CX), F32)
        inverse = 1.0 / (1.0 + below + above - below * ratio)
        ratio = above * inverse
        solve_coef[0, k] = inverse
        solve_coef[1, k] = below * inverse
        solve_coef[2, k] = ratio
        gain = inverse if k == 0 else below * inverse * gain
        gains.append(gain)
        ratios.append(ratio)
    value = jnp.zeros((CY, CX), F32)
    for k in reversed(range(LEV)):
        value = gains[k] + ratios[k] * value
        gain_ref[k] = value * rate_ref[...]

    for copy in halos:
        copy.wait_recv()
    mid = (place >= 8) & (place < 12)
    sides = ([], [])
    for c, k in planes:
        e = c * 8 + k
        own = cpacked[c, k]
        from_left = replicate(jnp.where(lanes < 4, roll_lanes(halo_in[0, 6], -4 * e), 0.0))
        from_right = replicate(jnp.where(mid & (lanes < 16), roll_lanes(halo_in[1, 6], 8 - 4 * e), 0.0))
        strip_coef[0, k >> 2, k & 3, c] = jnp.where(place < 4, from_left, roll_lanes(own, -4))
        strip_coef[1, k >> 2, k & 3, c] = jnp.where(mid, from_right, own)
    for k in range(LEV):
        for side in range(2):
            held = strip_coef.at[side, k >> 2, k & 3]
            for n, value in enumerate(stencil_coefs(held[0], held[1])):
                held[n] = value

    for p in range(3 * LEV):
        n, t = p >> 2, p & 3
        own = packed[p]
        strips[0, p // 12, p % 12] = jnp.where(
            place < 4, roll_lanes(halo_in[0, n], -4 * t), roll_lanes(own, -4)
        )
        strips[1, p // 12, p % 12] = jnp.where(mid, roll_lanes(halo_in[1, n], 8 - 4 * t), own)

    def strip_step(n, carry):
        half = n >> 2
        for j in range(4):
            for side in range(2):
                coefs = [strip_coef[side, half, j, i] for i in range(5)]
                for m in range(3):
                    p = j * 3 + m
                    strips[side, half, p] = one_step(strips[side, half, p], coefs)
        return carry

    lax.fori_loop(0, 8, strip_step, 0)
    for p in range(3 * LEV):
        h, r = p // 12, p % 12
        packed[p] = jnp.where(place < 4, roll_lanes(strips[1, h, r], -4), strips[0, h, r])

    edge = (lanes < 4) | (lanes >= CX - 4)

    def solve_fields(n, carry):
        m = n >> 1
        for j in range(4):
            f = n * 4 + j
            turn = CX - 4 - 16 * ((n & 1) * 4 + j)
            solved = jnp.zeros((CY, CX), F32)
            kept = []
            for k in range(LEV):
                value = jnp.where(edge, pltpu.roll(packed[k * 3 + m], turn, 1), state[k, f])
                solved = solve_coef[0, k] * value + solve_coef[1, k] * solved
                kept.append(solved)
            upper = kept[-1]
            state[LEV - 1, f] = upper
            for k in reversed(range(LEV - 1)):
                upper = kept[k] + solve_coef[2, k] * upper
                state[k, f] = upper
        return carry

    lax.fori_loop(0, FIELDS // 4, solve_fields, 0)
    store = pltpu.make_async_copy(state, solved_hbm, store_sem)
    store.start()

    for copy in scatters:
        copy.wait_recv()
    for g in range(GROUPS):
        total = arrived[g, 0].astype(F32)
        for d in range(1, 4):
            total = total + arrived[g, d].astype(F32)
        incoming_ref[g * GF : (g + 1) * GF] = total

    for g in range(GROUPS):
        for copy in gathers[g]:
            copy.wait_send()
    for copy in halos:
        copy.wait_send()
    for copy in scatters:
        copy.wait_send()
    store.wait()


def per_device(
    state_field,
    courant,
    diffusivity,
    coupling_rate,
    weight_table,
    source_row,
    destination_tile_ids,
    dest_row,
    weight_slot,
):
    vmem, hbm = pl.BlockSpec(memory_space=pltpu.VMEM), pl.BlockSpec(memory_space=pltpu.HBM)
    plane = (CY, CX)
    solved, gain, incoming = pl.pallas_call(
        kernel,
        out_shape=(
            jax.ShapeDtypeStruct((LEV, FIELDS) + plane, F32),
            jax.ShapeDtypeStruct((LEV,) + plane, F32),
            jax.ShapeDtypeStruct((FIELDS,) + plane, F32),
        ),
        in_specs=[hbm] * 9,
        out_specs=(hbm, vmem, vmem),
        scratch_shapes=[
            pltpu.VMEM((LEV, FIELDS) + plane, F32),
            pltpu.VMEM((2, LEV) + plane, F32),
            pltpu.VMEM((LEV,) + plane, F32),
            pltpu.VMEM(plane, F32),
            pltpu.VMEM((4, ENTRIES), I32),
            pltpu.VMEM((WTAB, CX, CX), BF16),
            pltpu.VMEM((24,) + plane, F32),
            pltpu.VMEM((2, LEV) + plane, F32),
            pltpu.VMEM((2, 2, 12) + plane, F32),
            pltpu.VMEM((2, 2, 4, 5) + plane, F32),
            pltpu.VMEM((2, 7) + plane, F32),
            pltpu.VMEM((2, 7) + plane, F32),
            pltpu.VMEM((LEV, 5) + plane, F32),
            pltpu.VMEM((GROUPS, 4, 4, SLABS) + plane, BF16),
            pltpu.VMEM((4, WTAB * CY, 256), BF16),
            pltpu.VMEM((4, WTAB, GF * CY, CX), BF16),
            pltpu.VMEM((GROUPS, 4, GF) + plane, BF16),
            pltpu.VMEM((GROUPS, 4, GF) + plane, BF16),
            pltpu.VMEM((3, LEV) + plane, F32),
            pltpu.SemaphoreType.DMA((LEV,)),
            pltpu.SemaphoreType.DMA((4,)),
            pltpu.SemaphoreType.DMA((4,)),
            pltpu.SemaphoreType.DMA,
            pltpu.SemaphoreType.DMA((GROUPS, 14)),
            pltpu.SemaphoreType.DMA((GROUPS, 14)),
            pltpu.SemaphoreType.DMA((2,)),
            pltpu.SemaphoreType.DMA((2,)),
            pltpu.SemaphoreType.DMA((GROUPS, 4)),
            pltpu.SemaphoreType.DMA((GROUPS, 4)),
        ],
        compiler_params=pltpu.CompilerParams(
            collective_id=0, has_side_effects=True, vmem_limit_bytes=60 * 2**20
        ),
        name="interval",
    )(
        state_field[0],
        courant[0],
        diffusivity[0],
        coupling_rate[0],
        weight_table,
        source_row[0],
        destination_tile_ids.reshape(1, ENTRIES),
        dest_row[0],
        weight_slot[0],
    )
    return (solved + gain[:, None] * incoming[None])[None]


def solution(mesh):
    return jax.shard_map(
        per_device,
        mesh=mesh,
        in_specs=(
            P("comp", None, None, None, "tile"),
            P("comp", None, None, None, "tile"),
            P("comp", None, None, "tile"),
            P("comp", None, "tile"),
            P(),
            P("comp", "tile", None),
            P("comp", "tile", None, None),
            P("comp", "tile", None),
            P("comp", "tile", None),
        ),
        out_specs=P("comp", None, None, None, "tile"),
        check_vma=False,
    )
```

time: 64.1 us -> 48.2 us (0.75)
  the two profiles are of different devices: /device:TPU:1 before, /device:TPU:0 now
where the time goes in v1:
time: 48.2 us; the launch traced here: 48 us
  Pallas kernels  45.1 us (94%)
  other arithmetic  2.86 us (6%)
    pallas_call x1, Pallas kernels, per_device(): pl.pallas_call(kernel, out_shape=(jax.ShapeDtypeStruct((LEV, FIELDS) + pl...  45.1 us
    broadcast_in_dim x1, other arithmetic, per_device(): return (solved + gain[:, None] * incoming[None])[None]  2.86 us

profile of v1, /device:TPU:0, one launch (start us, length us, event | category | flops | bytes accessed | tf_op | source)
XLA Modules:
  0.0 48.0 jit_solution(9946489976873859950)
XLA Ops:
  0.0 45.1 %interval.1 = (f32[8,24,16,128]{3,2,1,0:T(8,128)}, f32[8,16,128]{2,1,0:T(8,128)}, f32[24,16,128]{2,1,0:T(8,128)}) custom-call(f32[8,24,16,128]{3,2,1,0:T(8,128)} %bitcast.10, f32[2,8,16,128]{3,2,1,0:T(8,128)} %bitcast.11, f32[8,16,128]{2,1,0:T(8,128)} %bitcast.12, f32[16,128]{1,0:T(8,128)} %bitcast.13, bf16[32,128,128]{2,1,0:T(8,128)(2,1)} %weight_hbm.1, ...), custom_call_target="tpu_custom_call" | custom-call | tf_op jit(solution)/shard_map/interval/pallas_call | solution.py:444
  45.2 2.9 %add_bitcast_fusion = f32[1,8,24,16,128]{4,3,2,1,0:T(8,128)} fusion(f32[8,24,16,128]{3,2,1,0:T(8,128)} %get-tuple-element.8, f32[24,16,128]{2,1,0:T(8,128)} %get-tuple-element.10, f32[8,16,128]{2,1,0:T(8,128)} %get-tuple-element.9), kind=kLoop, calls=%fused_computation | loop fusion | flops 786432 | bytes 3407872 | tf_op jit(solution)/shard_map/broadcast_in_dim | solution.py:499

commit v2 on v1

--- a/solution.py
+++ b/solution.py
@@ -12,8 +12,8 @@
 ENTRIES, WTAB = 384, 32
 GROUPS = 3
 GF = FIELDS // GROUPS
-SLABS = GF + 1
-STRIDE = (16, 4, 1)
+HALF = GF // 2
+SLABS = HALF + 1
 AXES = ((0, 1, 2), (1, 2, 0), (2, 0, 1))
 F32, BF16, I32 = jnp.float32, jnp.bfloat16, jnp.int32
 
@@ -101,7 +101,9 @@
     coords = (tile >> 4, (tile >> 2) & 3, tile & 3)
 
     def shifted(axis, step):
-        return tile + (((coords[axis] + step) & 3) - coords[axis]) * STRIDE[axis]
+        place = 4 - 2 * axis
+        here = (tile >> place) & 3
+        return tile + ((((here + step) & 3) - here) << place)
 
     right, left = (tile + 1) & 63, (tile + 63) & 63
     barrier = pltpu.get_barrier_semaphore()
@@ -152,11 +154,13 @@
         hot = (iota((CX, ENTRIES), 0) == spot).astype(F32).astype(BF16)
         kept = jnp.where((quarter == rel[q]) & (kind < 3), values, 0)
         table = lax.dot_general(kept.astype(F32).astype(BF16), hot, NT, preferred_element_type=F32)
-        gath[g, 0, 0, GF] = table.astype(BF16)
+        gath[0, g, 0, 0, HALF] = table.astype(BF16)
 
     loads[0].wait()
-    for g in range(GROUPS):
-        gath[g, 0, 0, :GF] = state[0, g * GF : (g + 1) * GF].astype(BF16)
+    for h in range(2):
+        for g in range(GROUPS):
+            start = (g * 2 + h) * HALF
+            gath[h, g, 0, 0, :HALF] = state[0, start : start + HALF].astype(BF16)
 
     pl.semaphore_wait(barrier, len(greeted))
 
@@ -170,19 +174,21 @@
             device_id_type=MESH,
         )
 
-    def gather_copy(g, number):
-        u, v, q = AXES[g]
-        block = lambda i, j: gath.at[g, i, j]
-        low, high = pl.ds(0, 5), pl.ds(5, SLABS - 5)
+    def gather_copy(h, g, number):
+        slabs = SLABS - h
+        cut = 3 - h
+        every, low, high = pl.ds(0, slabs), pl.ds(0, cut), pl.ds(cut, slabs - cut)
+        block = lambda i, j, part=every: gath.at[h, g, i, j, part]
+        u, v = g, (g + 1) % 3
         src, dst, axis, step = (
             (block(0, 0), block(0, 2), u, 1),
             (block(0, 0), block(0, 1), u, 3),
             (block(0, 0), block(2, 0), v, 1),
             (block(0, 0), block(1, 0), v, 3),
-            (gath.at[g, 0, 2, low], gath.at[g, 0, 3, low], u, 1),
-            (gath.at[g, 0, 1, high], gath.at[g, 0, 3, high], u, 3),
-            (gath.at[g, 0, pl.ds(1, 2)], gath.at[g, 2, pl.ds(1, 2)], v, 1),
-            (gath.at[g, 0, pl.ds(1, 2)], gath.at[g, 1, pl.ds(1, 2)], v, 3),
+            (block(0, 2, low), block(0, 3, low), u, 1),
+            (block(0, 1, high), block(0, 3, high), u, 3),
+            (block(0, pl.ds(1, 2)), block(2, pl.ds(1, 2)), v, 1),
+            (block(0, pl.ds(1, 2)), block(1, pl.ds(1, 2)), v, 3),
             (block(2, 0), block(3, 0), v, 1),
             (block(0, 3), block(2, 3), v, 1),
             (block(0, 3), block(1, 3), v, 3),
@@ -190,22 +196,25 @@
             (block(1, 2), block(3, 2), v, 3),
             (block(1, 3), block(3, 3), v, 3),
         )[number]
-        return remote(src, dst, ag_send.at[g, number], ag_recv.at[g, number], (comp, shifted(axis, step)))
-
-    gathers = [[gather_copy(g, number) for number in range(14)] for g in range(GROUPS)]
-    rounds = ((0, 1, 2, 3), (4, 5, 6, 7, 8), (9, 10, 11, 12), (13,))
-
-    def start_round(n):
-        for number in rounds[n]:
-            for g in range(GROUPS):
-                gathers[g][number].start()
-
-    def wait_round(n):
-        for number in rounds[n]:
-            for g in range(GROUPS):
-                gathers[g][number].wait_recv()
-
-    start_round(0)
+        return remote(
+            src, dst, ag_send.at[h, g, number], ag_recv.at[h, g, number], (comp, shifted(axis, step))
+        )
+
+    def after(h, g, *moves):
+        for waited, started in moves:
+            for number in waited:
+                gather_copy(h, g, number).wait_recv()
+            for number in started:
+                gather_copy(h, g, number).start()
+
+    first = (((), (0, 1, 2, 3)),)
+    second = (((0, 1), (4, 5, 6, 7)), ((2,), (8,)))
+    third = (((4, 5), (9, 10)), ((6,), (11,)), ((7,), (12,)))
+    fourth = (((10,), (13,)),)
+    rest = (((3, 8, 9, 11, 12, 13), ()),)
+
+    for g in range(GROUPS):
+        after(0, g, *first)
 
     for load in loads[1:]:
         load.wait()
@@ -245,85 +254,138 @@
     for copy in halos:
         copy.start()
 
-    wait_round(0)
-    start_round(1)
-
-    def coef_level(k, carry):
+    for g in range(GROUPS):
+        after(0, g, *second)
+    for g in range(GROUPS):
+        after(1, g, *first)
+
+    def level_coefs(k, carry):
         for n, value in enumerate(stencil_coefs(courant_ref[0, k], courant_ref[1, k])):
             coef[k, n] = value
         return carry
 
     for k in range(LEV):
-        coef_level(k, 0)
+        level_coefs(k, 0)
+
+    for copy in halos:
+        copy.wait_recv()
+    mid = (place >= 8) & (place < 12)
+    for c, k in planes:
+        e = c * 8 + k
+        own = cpacked[c, k]
+        from_left = replicate(jnp.where(lanes < 4, roll_lanes(halo_in[0, 6], -4 * e), 0.0))
+        from_right = replicate(jnp.where(mid & (lanes < 16), roll_lanes(halo_in[1, 6], 8 - 4 * e), 0.0))
+        strip_coef[0, k >> 2, k & 3, c] = jnp.where(place < 4, from_left, roll_lanes(own, -4))
+        strip_coef[1, k >> 2, k & 3, c] = jnp.where(mid, from_right, own)
+
+    for g in range(GROUPS):
+        after(0, g, *third)
+    for g in range(GROUPS):
+        after(1, g, *second)
+
+    for k in range(LEV):
+        for side in range(2):
+            held = strip_coef.at[side, k >> 2, k & 3]
+            for n, value in enumerate(stencil_coefs(held[0], held[1])):
+                held[n] = value
+    for p in range(3 * LEV):
+        n, t = p >> 2, p & 3
+        own = packed[p]
+        strips[0, p // 12, p % 12] = jnp.where(
+            place < 4, roll_lanes(halo_in[0, n], -4 * t), roll_lanes(own, -4)
+        )
+        strips[1, p // 12, p % 12] = jnp.where(mid, roll_lanes(halo_in[1, n], 8 - 4 * t), own)
+
+    for g in range(GROUPS):
+        after(0, g, *fourth)
+
+    def strip_step(n, carry):
+        half = n >> 2
+        for j in range(4):
+            for side in range(2):
+                coefs = [strip_coef[side, half, j, i] for i in range(5)]
+                for m in range(3):
+                    p = j * 3 + m
+                    strips[side, half, p] = one_step(strips[side, half, p], coefs)
+        return carry
+
+    lax.fori_loop(0, 8, strip_step, 0)
+    for p in range(3 * LEV):
+        i, r = p // 12, p % 12
+        packed[p] = jnp.where(place < 4, roll_lanes(strips[1, i, r], -4), strips[0, i, r])
 
     def transport_step(n, carry):
         k = n >> 2
-        coefs = [coef[k, n] for n in range(5)]
+        coefs = [coef[k, i] for i in range(5)]
         for f in range(FIELDS):
             state[k, f] = one_step(state[k, f], coefs)
         return carry
 
-    lax.fori_loop(0, 4, transport_step, 0)
-    wait_round(1)
-    start_round(2)
-    lax.fori_loop(4, 16, transport_step, 0)
-    wait_round(2)
-    start_round(3)
-    lax.fori_loop(16, 32, transport_step, 0)
+    def transport_level(k):
+        coefs = [coef[k, i] for i in range(5)]
+        for step in range(4):
+            for f in range(FIELDS):
+                state[k, f] = one_step(state[k, f], coefs)
 
     small_loads[3].wait()
-    wait_round(3)
     rows_p, rows_q = iota((WTAB * CY, CX), 0), iota((256, CX), 0)
     lane_p = iota((1, CX), 1) >> 3
-    scatters = []
-    for g, (u, v, q) in enumerate(AXES):
-        table = jnp.zeros((CY, CX), F32)
-        for p in range(16):
-            rv, ru = ORDER[p // 4], ORDER[p % 4]
-            offset = ((-ru % 4) * 4 + (-rv % 4)) * 8
-            moved = roll_lanes(gath[g, p // 4, p % 4, GF].astype(F32), p * 8 - offset)
-            table = jnp.where((lanes >> 3) == p, moved, table)
-        codes = table.astype(I32)
+
+    def scatter_copy(h, g, d):
+        target = (1 - comp, tile if d == 0 else shifted((g + 2) % 3, d))
+        return remote(
+            outgoing.at[h, g, d],
+            arrived.at[h, g, (4 - d) % 4],
+            sc_send.at[h, g, d],
+            sc_recv.at[h, g, d],
+            target,
+        )
+
+    def remap(h, g, carry):
+        after(h, g, *rest)
+        if h == 0:
+            after(1, g, *third)
+            table = jnp.zeros((CY, CX), F32)
+            for p in range(16):
+                rv, ru = ORDER[p // 4], ORDER[p % 4]
+                offset = ((-ru % 4) * 4 + (-rv % 4)) * 8
+                moved = roll_lanes(gath[0, g, p // 4, p % 4, HALF].astype(F32), p * 8 - offset)
+                table = jnp.where((lanes >> 3) == p, moved, table)
+            codes = table.astype(I32)
+            for d in range(4):
+                w_e, r_e, y_e = codes[d : d + 1], codes[4 + d : 5 + d], codes[8 + d : 9 + d]
+                into = (rows_p == jnp.where(y_e > 0, w_e * CY + y_e - 1, -1)).astype(F32).astype(BF16)
+                outof = (rows_q == lane_p * CY + r_e).astype(F32).astype(BF16)
+                pick[g, d] = lax.dot_general(into, outof, NT, preferred_element_type=F32).astype(BF16)
+        blocks = [
+            jnp.concatenate(
+                [gath[h, g, :, :, 2 * pair + i].reshape(256, CX) for i in range(2)], axis=1
+            )
+            for pair in range(HALF // 2)
+        ]
         for d in range(4):
-            w_e, r_e, y_e = codes[d : d + 1], codes[4 + d : 5 + d], codes[8 + d : 9 + d]
-            into = (rows_p == jnp.where(y_e > 0, w_e * CY + y_e - 1, -1)).astype(F32).astype(BF16)
-            outof = (rows_q == lane_p * CY + r_e).astype(F32).astype(BF16)
-            pick[d] = lax.dot_general(into, outof, NT, preferred_element_type=F32).astype(BF16)
-
-        def spread_quarter(d, carry):
-            chosen = pick[d]
-            for pair in range(GF // 2):
-                blocks = jnp.concatenate(
-                    [gath[g, :, :, 2 * pair + h].reshape(256, CX) for h in range(2)], axis=1
-                )
-                summed = jnp.dot(chosen, blocks, preferred_element_type=F32).astype(BF16)
-                for h in range(2):
+            for pair in range(HALF // 2):
+                summed = jnp.dot(pick[g, d], blocks[pair], preferred_element_type=F32).astype(BF16)
+                for i in range(2):
                     for w in range(WTAB):
-                        spread[d, w, pl.ds((2 * pair + h) * CY, CY)] = summed[
-                            w * CY : (w + 1) * CY, h * CX : (h + 1) * CX
-                        ]
-            return carry
-
-        lax.fori_loop(0, 4, spread_quarter, 0)
+                        row = (d * HALF + 2 * pair + i) * CY
+                        spread[w, row : row + CY] = summed[w * CY : (w + 1) * CY, i * CX : (i + 1) * CX]
+        transport_level(3 * h + g)
+        if h == 0:
+            after(1, g, *fourth)
         table_all = jnp.concatenate([weight[w] for w in range(WTAB)], axis=1)
-        for d2 in range(2):
-            chosen = jnp.concatenate(
-                [
-                    jnp.concatenate([spread[2 * d2, w], spread[2 * d2 + 1, w]], axis=0)
-                    for w in range(WTAB)
-                ],
-                axis=1,
-            )
-            result = lax.dot_general(chosen, table_all, NT, preferred_element_type=F32).astype(BF16)
-            for h in range(2):
-                outgoing[g, 2 * d2 + h] = result[h * 128 : (h + 1) * 128].reshape(GF, CY, CX)
+        chosen = jnp.concatenate([spread[w] for w in range(WTAB)], axis=1)
+        result = lax.dot_general(chosen, table_all, NT, preferred_element_type=F32).astype(BF16)
         for d in range(4):
-            target = (1 - comp, tile if d == 0 else shifted(q, d))
-            copy = remote(
-                outgoing.at[g, d], arrived.at[g, (4 - d) % 4], sc_send.at[g, d], sc_recv.at[g, d], target
-            )
-            copy.start()
-            scatters.append(copy)
+            rows = HALF * CY
+            outgoing[h, g, d] = result[d * rows : (d + 1) * rows].reshape(HALF, CY, CX)
+        for d in range(4):
+            scatter_copy(h, g, d).start()
+        return carry
+
+    for h in range(2):
+        lax.fori_loop(0, GROUPS, lambda g, carry, h=h: remap(h, g, carry), 0)
+    lax.fori_loop(24, 32, transport_step, 0)
 
     small_loads[1].wait()
     small_loads[2].wait()
@@ -346,46 +408,6 @@
         value = gains[k] + ratios[k] * value
         gain_ref[k] = value * rate_ref[...]
 
-    for copy in halos:
-        copy.wait_recv()
-    mid = (place >= 8) & (place < 12)
-    sides = ([], [])
-    for c, k in planes:
-        e = c * 8 + k
-        own = cpacked[c, k]
-        from_left = replicate(jnp.where(lanes < 4, roll_lanes(halo_in[0, 6], -4 * e), 0.0))
-        from_right = replicate(jnp.where(mid & (lanes < 16), roll_lanes(halo_in[1, 6], 8 - 4 * e), 0.0))
-        strip_coef[0, k >> 2, k & 3, c] = jnp.where(place < 4, from_left, roll_lanes(own, -4))
-        strip_coef[1, k >> 2, k & 3, c] = jnp.where(mid, from_right, own)
-    for k in range(LEV):
-        for side in range(2):
-            held = strip_coef.at[side, k >> 2, k & 3]
-            for n, value in enumerate(stencil_coefs(held[0], held[1])):
-                held[n] = value
-
-    for p in range(3 * LEV):
-        n, t = p >> 2, p & 3
-        own = packed[p]
-        strips[0, p // 12, p % 12] = jnp.where(
-            place < 4, roll_lanes(halo_in[0, n], -4 * t), roll_lanes(own, -4)
-        )
-        strips[1, p // 12, p % 12] = jnp.where(mid, roll_lanes(halo_in[1, n], 8 - 4 * t), own)
-
-    def strip_step(n, carry):
-        half = n >> 2
-        for j in range(4):
-            for side in range(2):
-                coefs = [strip_coef[side, half, j, i] for i in range(5)]
-                for m in range(3):
-                    p = j * 3 + m
-                    strips[side, half, p] = one_step(strips[side, half, p], coefs)
-        return carry
-
-    lax.fori_loop(0, 8, strip_step, 0)
-    for p in range(3 * LEV):
-        h, r = p // 12, p % 12
-        packed[p] = jnp.where(place < 4, roll_lanes(strips[1, h, r], -4), strips[0, h, r])
-
     edge = (lanes < 4) | (lanes >= CX - 4)
 
     def solve_fields(n, carry):
@@ -410,22 +432,43 @@
     store = pltpu.make_async_copy(state, solved_hbm, store_sem)
     store.start()
 
-    for copy in scatters:
-        copy.wait_recv()
-    for g in range(GROUPS):
-        total = arrived[g, 0].astype(F32)
-        for d in range(1, 4):
-            total = total + arrived[g, d].astype(F32)
-        incoming_ref[g * GF : (g + 1) * GF] = total
-
-    for g in range(GROUPS):
-        for copy in gathers[g]:
-            copy.wait_send()
+    for h in range(2):
+        for g in range(GROUPS):
+            for d in range(4):
+                scatter_copy(h, g, d).wait_recv()
+            total = arrived[h, g, 0].astype(F32)
+            for d in range(1, 4):
+                total = total + arrived[h, g, d].astype(F32)
+            start = (g * 2 + h) * HALF
+            incoming_ref[start : start + HALF] = total
+
+    def finish(g, carry):
+        for h in range(2):
+            for number in range(14):
+                gather_copy(h, g, number).wait_send()
+            for d in range(4):
+                scatter_copy(h, g, d).wait_send()
+        return carry
+
+    lax.fori_loop(0, GROUPS, finish, 0)
     for copy in halos:
         copy.wait_send()
-    for copy in scatters:
-        copy.wait_send()
     store.wait()
+
+
+def combine(solved_hbm, gain_ref, incoming_ref, out_hbm, held, load_sem, store_sem):
+    loads = [pltpu.make_async_copy(solved_hbm.at[k], held.at[k], load_sem.at[k]) for k in range(LEV)]
+    stores = [pltpu.make_async_copy(held.at[k], out_hbm.at[k], store_sem.at[k]) for k in range(LEV)]
+    for load in loads:
+        load.start()
+    for k in range(LEV):
+        loads[k].wait()
+        gain = gain_ref[k]
+        for f in range(FIELDS):
+            held[k, f] = held[k, f] + gain * incoming_ref[f]
+        stores[k].start()
+    for store in stores:
+        store.wait()
 
 
 def per_device(
@@ -464,22 +507,22 @@
             pltpu.VMEM((2, 7) + plane, F32),
             pltpu.VMEM((2, 7) + plane, F32),
             pltpu.VMEM((LEV, 5) + plane, F32),
-            pltpu.VMEM((GROUPS, 4, 4, SLABS) + plane, BF16),
-            pltpu.VMEM((4, WTAB * CY, 256), BF16),
-            pltpu.VMEM((4, WTAB, GF * CY, CX), BF16),
-            pltpu.VMEM((GROUPS, 4, GF) + plane, BF16),
-            pltpu.VMEM((GROUPS, 4, GF) + plane, BF16),
+            pltpu.VMEM((2, GROUPS, 4, 4, SLABS) + plane, BF16),
+            pltpu.VMEM((GROUPS, 4, WTAB * CY, 256), BF16),
+            pltpu.VMEM((WTAB, 4 * HALF * CY, CX), BF16),
+            pltpu.VMEM((2, GROUPS, 4, HALF) + plane, BF16),
+            pltpu.VMEM((2, GROUPS, 4, HALF) + plane, BF16),
             pltpu.VMEM((3, LEV) + plane, F32),
             pltpu.SemaphoreType.DMA((LEV,)),
             pltpu.SemaphoreType.DMA((4,)),
             pltpu.SemaphoreType.DMA((4,)),
             pltpu.SemaphoreType.DMA,
-            pltpu.SemaphoreType.DMA((GROUPS, 14)),
-            pltpu.SemaphoreType.DMA((GROUPS, 14)),
+            pltpu.SemaphoreType.DMA((2, GROUPS, 14)),
+            pltpu.SemaphoreType.DMA((2, GROUPS, 14)),
             pltpu.SemaphoreType.DMA((2,)),
             pltpu.SemaphoreType.DMA((2,)),
-            pltpu.SemaphoreType.DMA((GROUPS, 4)),
-            pltpu.SemaphoreType.DMA((GROUPS, 4)),
+            pltpu.SemaphoreType.DMA((2, GROUPS, 4)),
+            pltpu.SemaphoreType.DMA((2, GROUPS, 4)),
         ],
         compiler_params=pltpu.CompilerParams(
             collective_id=0, has_side_effects=True, vmem_limit_bytes=60 * 2**20
@@ -496,7 +539,20 @@
         dest_row[0],
         weight_slot[0],
     )
-    return (solved + gain[:, None] * incoming[None])[None]
+    out = pl.pallas_call(
+        combine,
+        out_shape=jax.ShapeDtypeStruct((LEV, FIELDS) + plane, F32),
+        in_specs=[hbm, vmem, vmem],
+        out_specs=hbm,
+        scratch_shapes=[
+            pltpu.VMEM((LEV, FIELDS) + plane, F32),
+            pltpu.SemaphoreType.DMA((LEV,)),
+            pltpu.SemaphoreType.DMA((LEV,)),
+        ],
+        compiler_params=pltpu.CompilerParams(vmem_limit_bytes=60 * 2**20),
+        name="combine",
+    )(solved, gain, incoming)
+    return out[None]
 
 
 def solution(mesh):

time: 48.2 us -> 51.1 us (1.060)
  the two profiles are of different devices: /device:TPU:0 before, /device:TPU:1 now
where the time goes in v2:
time: 51.1 us; the launch traced here: 50.9 us
  Pallas kernels  50.9 us (100%)
    pallas_call x1, Pallas kernels, per_device(): pl.pallas_call(kernel, out_shape=(jax.ShapeDtypeStruct((LEV, FIELDS) + pl...  47.6 us
    pallas_call x1, Pallas kernels, per_device(): pl.pallas_call(combine, out_shape=jax.ShapeDtypeStruct((LEV, FIELDS) + pl...  3.28 us

profile of v2, /device:TPU:1, one launch (start us, length us, event | category | flops | bytes accessed | tf_op | source)
XLA Modules:
  0.0 50.9 jit_solution(17294852560592599010)
XLA Ops:
  0.0 47.6 %interval.1 = (f32[8,24,16,128]{3,2,1,0:T(8,128)}, f32[8,16,128]{2,1,0:T(8,128)}, f32[24,16,128]{2,1,0:T(8,128)}) custom-call(f32[8,24,16,128]{3,2,1,0:T(8,128)} %bitcast.9, f32[2,8,16,128]{3,2,1,0:T(8,128)} %bitcast.10, f32[8,16,128]{2,1,0:T(8,128)} %bitcast.11, f32[16,128]{1,0:T(8,128)} %bitcast.12, bf16[32,128,128]{2,1,0:T(8,128)(2,1)} %weight_hbm.1, ...), custom_call_target="tpu_custom_call" | custom-call | tf_op jit(solution)/shard_map/interval/pallas_call | solution.py:487
  47.6 3.3 %combine.1 = f32[8,24,16,128]{3,2,1,0:T(8,128)} custom-call(f32[8,24,16,128]{3,2,1,0:T(8,128)} %get-tuple-element.8.solved_hbm, f32[8,16,128]{2,1,0:T(8,128)} %get-tuple-element.9.gain_ref, f32[24,16,128]{2,1,0:T(8,128)} %get-tuple-element.10.incoming_ref), custom_call_target="tpu_custom_call" | custom-call | tf_op jit(solution)/shard_map/combine/pallas_call | solution.py:542

commit v3 on v2

--- a/solution.py
+++ b/solution.py
@@ -7,13 +7,11 @@
 
 MESH = pl.DeviceIdType.MESH
 NT = (((1,), (1,)), ((), ()))
-ORDER = (0, 1, 3, 2)
 LEV, FIELDS, CY, CX = 8, 24, 16, 128
 ENTRIES, WTAB = 384, 32
 GROUPS = 3
 GF = FIELDS // GROUPS
-HALF = GF // 2
-SLABS = HALF + 1
+SLABS = GF + 1
 AXES = ((0, 1, 2), (1, 2, 0), (2, 0, 1))
 F32, BF16, I32 = jnp.float32, jnp.bfloat16, jnp.int32
 
@@ -46,12 +44,6 @@
         + north * pltpu.roll(a, CY - 1, 0)
         + south * pltpu.roll(a, 1, 0)
     )
-
-
-def replicate(value):
-    for shift in (16, 32, 64):
-        value = value + roll_lanes(value, shift)
-    return value
 
 
 def kernel(
@@ -74,7 +66,6 @@
     entries,
     weight,
     packed,
-    cpacked,
     strips,
     strip_coef,
     halo_out,
@@ -107,7 +98,7 @@
 
     right, left = (tile + 1) & 63, (tile + 63) & 63
     barrier = pltpu.get_barrier_semaphore()
-    greeted = [(comp, shifted(axis, step)) for axis in range(3) for step in (1, 3)]
+    greeted = [(comp, shifted(axis, step)) for axis in range(3) for step in (1, 2, 3)]
     greeted += [(comp, right), (comp, left), (1 - comp, tile)]
     greeted += [(1 - comp, shifted(axis, step)) for axis in range(3) for step in (1, 2, 3)]
     for target in greeted:
@@ -154,13 +145,11 @@
         hot = (iota((CX, ENTRIES), 0) == spot).astype(F32).astype(BF16)
         kept = jnp.where((quarter == rel[q]) & (kind < 3), values, 0)
         table = lax.dot_general(kept.astype(F32).astype(BF16), hot, NT, preferred_element_type=F32)
-        gath[0, g, 0, 0, HALF] = table.astype(BF16)
+        gath[g, 0, 0, GF] = table.astype(BF16)
 
     loads[0].wait()
-    for h in range(2):
-        for g in range(GROUPS):
-            start = (g * 2 + h) * HALF
-            gath[h, g, 0, 0, :HALF] = state[0, start : start + HALF].astype(BF16)
+    for g in range(GROUPS):
+        gath[g, 0, 0, :GF] = state[0, g * GF : (g + 1) * GF].astype(BF16)
 
     pl.semaphore_wait(barrier, len(greeted))
 
@@ -174,47 +163,30 @@
             device_id_type=MESH,
         )
 
-    def gather_copy(h, g, number):
-        slabs = SLABS - h
-        cut = 3 - h
-        every, low, high = pl.ds(0, slabs), pl.ds(0, cut), pl.ds(cut, slabs - cut)
-        block = lambda i, j, part=every: gath.at[h, g, i, j, part]
+    def gather_copy(g, number):
         u, v = g, (g + 1) % 3
-        src, dst, axis, step = (
-            (block(0, 0), block(0, 2), u, 1),
-            (block(0, 0), block(0, 1), u, 3),
-            (block(0, 0), block(2, 0), v, 1),
-            (block(0, 0), block(1, 0), v, 3),
-            (block(0, 2, low), block(0, 3, low), u, 1),
-            (block(0, 1, high), block(0, 3, high), u, 3),
-            (block(0, pl.ds(1, 2)), block(2, pl.ds(1, 2)), v, 1),
-            (block(0, pl.ds(1, 2)), block(1, pl.ds(1, 2)), v, 3),
-            (block(2, 0), block(3, 0), v, 1),
-            (block(0, 3), block(2, 3), v, 1),
-            (block(0, 3), block(1, 3), v, 3),
-            (block(2, 1), block(3, 1), v, 1),
-            (block(1, 2), block(3, 2), v, 3),
-            (block(1, 3), block(3, 3), v, 3),
-        )[number]
+        block = lambda i, j: gath.at[g, i, j]
+        step = number % 3 + 1
+        there = 4 - step
+        others = pl.ds(1, 3)
+        src, dst, axis = (
+            (block(0, 0), block(0, there), u),
+            (block(0, 0), block(there, 0), v),
+            (block(0, others), block(there, others), v),
+        )[number // 3]
         return remote(
-            src, dst, ag_send.at[h, g, number], ag_recv.at[h, g, number], (comp, shifted(axis, step))
+            src, dst, ag_send.at[g, number], ag_recv.at[g, number], (comp, shifted(axis, step))
         )
 
-    def after(h, g, *moves):
-        for waited, started in moves:
-            for number in waited:
-                gather_copy(h, g, number).wait_recv()
-            for number in started:
-                gather_copy(h, g, number).start()
-
-    first = (((), (0, 1, 2, 3)),)
-    second = (((0, 1), (4, 5, 6, 7)), ((2,), (8,)))
-    third = (((4, 5), (9, 10)), ((6,), (11,)), ((7,), (12,)))
-    fourth = (((10,), (13,)),)
-    rest = (((3, 8, 9, 11, 12, 13), ()),)
-
-    for g in range(GROUPS):
-        after(0, g, *first)
+    for number in (0, 2, 1, 3, 5, 4):
+        for g in range(GROUPS):
+            gather_copy(g, number).start()
+
+    def pass_on(g):
+        for number in range(3):
+            gather_copy(g, number).wait_recv()
+        for number in (6, 8, 7):
+            gather_copy(g, number).start()
 
     for load in loads[1:]:
         load.wait()
@@ -232,21 +204,18 @@
 
     lax.fori_loop(0, LEV, pack_level, 0)
     planes = [(c, k) for c in range(2) for k in range(LEV)]
-    for c, k in planes:
-        cpacked[c, k] = replicate(jnp.where(lanes < 16, roll_lanes(courant_ref[c, k], 8), 0.0))
+    spare = [jnp.where(lanes < 16, roll_lanes(courant_ref[c, k], 8), 0.0) for c, k in planes]
+    for shift in (16, 32, 64):
+        spare = [value + roll_lanes(value, shift) for value in spare]
+    for e, value in enumerate(spare):
+        packed[24 + e] = value
     quad = (lanes >> 2) & 3
-    for n in range(6):
+    for n in range(10):
         for side, base in ((0, 4), (1, 8)):
             value = roll_lanes(packed[4 * n], -base)
             for t in range(1, 4):
                 value = jnp.where(quad == t, roll_lanes(packed[4 * n + t], 4 * t - base), value)
             halo_out[side, n] = value
-    for side, base in ((0, 4), (1, 8)):
-        value = roll_lanes(cpacked[0, 0], -base)
-        for e in range(1, 16):
-            moved = roll_lanes(cpacked[e // 8, e % 8], 4 * (e % 4) - base)
-            value = jnp.where((lanes >> 2) == e, moved, value)
-        halo_out[side, 6] = value
     halos = [
         remote(halo_out.at[side], halo_in.at[side], halo_send.at[side], halo_recv.at[side], (comp, target))
         for side, target in ((0, right), (1, left))
@@ -254,11 +223,6 @@
     for copy in halos:
         copy.start()
 
-    for g in range(GROUPS):
-        after(0, g, *second)
-    for g in range(GROUPS):
-        after(1, g, *first)
-
     def level_coefs(k, carry):
         for n, value in enumerate(stencil_coefs(courant_ref[0, k], courant_ref[1, k])):
             coef[k, n] = value
@@ -267,37 +231,40 @@
     for k in range(LEV):
         level_coefs(k, 0)
 
+    def transport_step(n, carry):
+        k = n >> 2
+        coefs = [coef[k, i] for i in range(5)]
+        for f in range(FIELDS):
+            state[k, f] = one_step(state[k, f], coefs)
+        return carry
+
+    def transport_level(k):
+        coefs = [coef[k, i] for i in range(5)]
+        for step in range(4):
+            for f in range(FIELDS):
+                state[k, f] = one_step(state[k, f], coefs)
+
+    for g in range(GROUPS):
+        pass_on(g)
+
     for copy in halos:
         copy.wait_recv()
     mid = (place >= 8) & (place < 12)
-    for c, k in planes:
-        e = c * 8 + k
-        own = cpacked[c, k]
-        from_left = replicate(jnp.where(lanes < 4, roll_lanes(halo_in[0, 6], -4 * e), 0.0))
-        from_right = replicate(jnp.where(mid & (lanes < 16), roll_lanes(halo_in[1, 6], 8 - 4 * e), 0.0))
-        strip_coef[0, k >> 2, k & 3, c] = jnp.where(place < 4, from_left, roll_lanes(own, -4))
-        strip_coef[1, k >> 2, k & 3, c] = jnp.where(mid, from_right, own)
-
-    for g in range(GROUPS):
-        after(0, g, *third)
-    for g in range(GROUPS):
-        after(1, g, *second)
-
+
+    def strip(side, p):
+        n, t = p >> 2, p & 3
+        if side == 0:
+            return jnp.where(place < 4, roll_lanes(halo_in[0, n], -4 * t), roll_lanes(packed[p], -4))
+        return jnp.where(mid, roll_lanes(halo_in[1, n], 8 - 4 * t), packed[p])
+
+    for p in range(3 * LEV):
+        for side in range(2):
+            strips[side, p // 12, p % 12] = strip(side, p)
     for k in range(LEV):
         for side in range(2):
-            held = strip_coef.at[side, k >> 2, k & 3]
-            for n, value in enumerate(stencil_coefs(held[0], held[1])):
-                held[n] = value
-    for p in range(3 * LEV):
-        n, t = p >> 2, p & 3
-        own = packed[p]
-        strips[0, p // 12, p % 12] = jnp.where(
-            place < 4, roll_lanes(halo_in[0, n], -4 * t), roll_lanes(own, -4)
-        )
-        strips[1, p // 12, p % 12] = jnp.where(mid, roll_lanes(halo_in[1, n], 8 - 4 * t), own)
-
-    for g in range(GROUPS):
-        after(0, g, *fourth)
+            values = stencil_coefs(strip(side, 24 + k), strip(side, 32 + k))
+            for n, value in enumerate(values):
+                strip_coef[side, k >> 2, k & 3, n] = value
 
     def strip_step(n, carry):
         half = n >> 2
@@ -314,78 +281,56 @@
         i, r = p // 12, p % 12
         packed[p] = jnp.where(place < 4, roll_lanes(strips[1, i, r], -4), strips[0, i, r])
 
-    def transport_step(n, carry):
-        k = n >> 2
-        coefs = [coef[k, i] for i in range(5)]
-        for f in range(FIELDS):
-            state[k, f] = one_step(state[k, f], coefs)
-        return carry
-
-    def transport_level(k):
-        coefs = [coef[k, i] for i in range(5)]
-        for step in range(4):
-            for f in range(FIELDS):
-                state[k, f] = one_step(state[k, f], coefs)
+    lax.fori_loop(12, 32, transport_step, 0)
 
     small_loads[3].wait()
     rows_p, rows_q = iota((WTAB * CY, CX), 0), iota((256, CX), 0)
     lane_p = iota((1, CX), 1) >> 3
 
-    def scatter_copy(h, g, d):
+    def scatter_copy(g, d):
         target = (1 - comp, tile if d == 0 else shifted((g + 2) % 3, d))
         return remote(
-            outgoing.at[h, g, d],
-            arrived.at[h, g, (4 - d) % 4],
-            sc_send.at[h, g, d],
-            sc_recv.at[h, g, d],
-            target,
+            outgoing.at[g, d], arrived.at[g, (4 - d) % 4], sc_send.at[g, d], sc_recv.at[g, d], target
         )
 
-    def remap(h, g, carry):
-        after(h, g, *rest)
-        if h == 0:
-            after(1, g, *third)
-            table = jnp.zeros((CY, CX), F32)
-            for p in range(16):
-                rv, ru = ORDER[p // 4], ORDER[p % 4]
-                offset = ((-ru % 4) * 4 + (-rv % 4)) * 8
-                moved = roll_lanes(gath[0, g, p // 4, p % 4, HALF].astype(F32), p * 8 - offset)
-                table = jnp.where((lanes >> 3) == p, moved, table)
-            codes = table.astype(I32)
-            for d in range(4):
-                w_e, r_e, y_e = codes[d : d + 1], codes[4 + d : 5 + d], codes[8 + d : 9 + d]
-                into = (rows_p == jnp.where(y_e > 0, w_e * CY + y_e - 1, -1)).astype(F32).astype(BF16)
-                outof = (rows_q == lane_p * CY + r_e).astype(F32).astype(BF16)
-                pick[g, d] = lax.dot_general(into, outof, NT, preferred_element_type=F32).astype(BF16)
-        blocks = [
-            jnp.concatenate(
-                [gath[h, g, :, :, 2 * pair + i].reshape(256, CX) for i in range(2)], axis=1
-            )
-            for pair in range(HALF // 2)
-        ]
+    def remap(g, carry):
+        for number in range(3, 9):
+            gather_copy(g, number).wait_recv()
+        table = jnp.zeros((CY, CX), F32)
+        for p in range(16):
+            rv, ru = p // 4, p % 4
+            offset = ((-ru % 4) * 4 + (-rv % 4)) * 8
+            moved = roll_lanes(gath[g, rv, ru, GF].astype(F32), p * 8 - offset)
+            table = jnp.where((lanes >> 3) == p, moved, table)
+        codes = table.astype(I32)
         for d in range(4):
-            for pair in range(HALF // 2):
-                summed = jnp.dot(pick[g, d], blocks[pair], preferred_element_type=F32).astype(BF16)
+            w_e, r_e, y_e = codes[d : d + 1], codes[4 + d : 5 + d], codes[8 + d : 9 + d]
+            into = (rows_p == jnp.where(y_e > 0, w_e * CY + y_e - 1, -1)).astype(F32).astype(BF16)
+            outof = (rows_q == lane_p * CY + r_e).astype(F32).astype(BF16)
+            pick[d] = lax.dot_general(into, outof, NT, preferred_element_type=F32).astype(BF16)
+        for d in range(4):
+            for pair in range(GF // 2):
+                blocks = jnp.concatenate(
+                    [gath[g, :, :, 2 * pair + i].reshape(256, CX) for i in range(2)], axis=1
+                )
+                summed = jnp.dot(pick[d], blocks, preferred_element_type=F32).astype(BF16)
                 for i in range(2):
                     for w in range(WTAB):
-                        row = (d * HALF + 2 * pair + i) * CY
+                        row = (d * GF + 2 * pair + i) * CY
                         spread[w, row : row + CY] = summed[w * CY : (w + 1) * CY, i * CX : (i + 1) * CX]
-        transport_level(3 * h + g)
-        if h == 0:
-            after(1, g, *fourth)
+        transport_level(g)
         table_all = jnp.concatenate([weight[w] for w in range(WTAB)], axis=1)
-        chosen = jnp.concatenate([spread[w] for w in range(WTAB)], axis=1)
-        result = lax.dot_general(chosen, table_all, NT, preferred_element_type=F32).astype(BF16)
+        rows = GF * CY
+        for d in range(0, 4, 2):
+            chosen = jnp.concatenate([spread[w, d * rows : (d + 2) * rows] for w in range(WTAB)], axis=1)
+            result = lax.dot_general(chosen, table_all, NT, preferred_element_type=F32).astype(BF16)
+            for i in range(2):
+                outgoing[g, d + i] = result[i * rows : (i + 1) * rows].reshape(GF, CY, CX)
         for d in range(4):
-            rows = HALF * CY
-            outgoing[h, g, d] = result[d * rows : (d + 1) * rows].reshape(HALF, CY, CX)
-        for d in range(4):
-            scatter_copy(h, g, d).start()
-        return carry
-
-    for h in range(2):
-        lax.fori_loop(0, GROUPS, lambda g, carry, h=h: remap(h, g, carry), 0)
-    lax.fori_loop(24, 32, transport_step, 0)
+            scatter_copy(g, d).start()
+        return carry
+
+    lax.fori_loop(0, GROUPS, remap, 0)
 
     small_loads[1].wait()
     small_loads[2].wait()
@@ -432,22 +377,19 @@
     store = pltpu.make_async_copy(state, solved_hbm, store_sem)
     store.start()
 
-    for h in range(2):
-        for g in range(GROUPS):
-            for d in range(4):
-                scatter_copy(h, g, d).wait_recv()
-            total = arrived[h, g, 0].astype(F32)
-            for d in range(1, 4):
-                total = total + arrived[h, g, d].astype(F32)
-            start = (g * 2 + h) * HALF
-            incoming_ref[start : start + HALF] = total
+    for g in range(GROUPS):
+        for d in range(4):
+            scatter_copy(g, d).wait_recv()
+        total = arrived[g, 0].astype(F32)
+        for d in range(1, 4):
+            total = total + arrived[g, d].astype(F32)
+        incoming_ref[g * GF : (g + 1) * GF] = total
 
     def finish(g, carry):
-        for h in range(2):
-            for number in range(14):
-                gather_copy(h, g, number).wait_send()
-            for d in range(4):
-                scatter_copy(h, g, d).wait_send()
+        for number in range(9):
+            gather_copy(g, number).wait_send()
+        for d in range(4):
+            scatter_copy(g, d).wait_send()
         return carry
 
     lax.fori_loop(0, GROUPS, finish, 0)
@@ -500,29 +442,28 @@
             pltpu.VMEM(plane, F32),
             pltpu.VMEM((4, ENTRIES), I32),
             pltpu.VMEM((WTAB, CX, CX), BF16),
-            pltpu.VMEM((24,) + plane, F32),
-            pltpu.VMEM((2, LEV) + plane, F32),
+            pltpu.VMEM((40,) + plane, F32),
             pltpu.VMEM((2, 2, 12) + plane, F32),
             pltpu.VMEM((2, 2, 4, 5) + plane, F32),
-            pltpu.VMEM((2, 7) + plane, F32),
-            pltpu.VMEM((2, 7) + plane, F32),
+            pltpu.VMEM((2, 10) + plane, F32),
+            pltpu.VMEM((2, 10) + plane, F32),
             pltpu.VMEM((LEV, 5) + plane, F32),
-            pltpu.VMEM((2, GROUPS, 4, 4, SLABS) + plane, BF16),
-            pltpu.VMEM((GROUPS, 4, WTAB * CY, 256), BF16),
-            pltpu.VMEM((WTAB, 4 * HALF * CY, CX), BF16),
-            pltpu.VMEM((2, GROUPS, 4, HALF) + plane, BF16),
-            pltpu.VMEM((2, GROUPS, 4, HALF) + plane, BF16),
+            pltpu.VMEM((GROUPS, 4, 4, SLABS) + plane, BF16),
+            pltpu.VMEM((4, WTAB * CY, 256), BF16),
+            pltpu.VMEM((WTAB, 4 * GF * CY, CX), BF16),
+            pltpu.VMEM((GROUPS, 4, GF) + plane, BF16),
+            pltpu.VMEM((GROUPS, 4, GF) + plane, BF16),
             pltpu.VMEM((3, LEV) + plane, F32),
             pltpu.SemaphoreType.DMA((LEV,)),
             pltpu.SemaphoreType.DMA((4,)),
             pltpu.SemaphoreType.DMA((4,)),
             pltpu.SemaphoreType.DMA,
-            pltpu.SemaphoreType.DMA((2, GROUPS, 14)),
-            pltpu.SemaphoreType.DMA((2, GROUPS, 14)),
+            pltpu.SemaphoreType.DMA((GROUPS, 9)),
+            pltpu.SemaphoreType.DMA((GROUPS, 9)),
             pltpu.SemaphoreType.DMA((2,)),
             pltpu.SemaphoreType.DMA((2,)),
-            pltpu.SemaphoreType.DMA((2, GROUPS, 4)),
-            pltpu.SemaphoreType.DMA((2, GROUPS, 4)),
+            pltpu.SemaphoreType.DMA((GROUPS, 4)),
+            pltpu.SemaphoreType.DMA((GROUPS, 4)),
         ],
         compiler_params=pltpu.CompilerParams(
             collective_id=0, has_side_effects=True, vmem_limit_bytes=60 * 2**20

time: 51.1 us -> 38.9 us (0.76)
  Pallas kernels: 50.9 us -> 38.7 us
    pallas_call x1, Pallas kernels: 47.6 us -> 35.4 us  [per_device(): pl.pallas_call(kernel, out_shape=(jax.ShapeDtypeStruct((LEV, FIELDS) + pl...]
where the time goes in v3:
time: 38.9 us; the launch traced here: 38.7 us
  Pallas kernels  38.7 us (99%)
    pallas_call x1, Pallas kernels, per_device(): pl.pallas_call(kernel, out_shape=(jax.ShapeDtypeStruct((LEV, FIELDS) + pl...  35.4 us
    pallas_call x1, Pallas kernels, per_device(): pl.pallas_call(combine, out_shape=jax.ShapeDtypeStruct((LEV, FIELDS) + pl...  3.28 us

profile of v3, /device:TPU:1, one launch (start us, length us, event | category | flops | bytes accessed | tf_op | source)
XLA Modules:
  0.0 38.7 jit_solution(2464424961144096698)
XLA Ops:
  0.0 35.4 %interval.1 = (f32[8,24,16,128]{3,2,1,0:T(8,128)}, f32[8,16,128]{2,1,0:T(8,128)}, f32[24,16,128]{2,1,0:T(8,128)}) custom-call(f32[8,24,16,128]{3,2,1,0:T(8,128)} %bitcast.9, f32[2,8,16,128]{3,2,1,0:T(8,128)} %bitcast.10, f32[8,16,128]{2,1,0:T(8,128)} %bitcast.11, f32[16,128]{1,0:T(8,128)} %bitcast.12, bf16[32,128,128]{2,1,0:T(8,128)(2,1)} %weight_hbm.1, ...), custom_call_target="tpu_custom_call" | custom-call | tf_op jit(solution)/shard_map/interval/pallas_call | solution.py:429
  35.4 3.3 %combine.1 = f32[8,24,16,128]{3,2,1,0:T(8,128)} custom-call(f32[8,24,16,128]{3,2,1,0:T(8,128)} %get-tuple-element.8.solved_hbm, f32[8,16,128]{2,1,0:T(8,128)} %get-tuple-element.9.gain_ref, f32[24,16,128]{2,1,0:T(8,128)} %get-tuple-element.10.incoming_ref), custom_call_target="tpu_custom_call" | custom-call | tf_op jit(solution)/shard_map/combine/pallas_call | solution.py:483

commit v4 on v3

--- a/solution.py
+++ b/solution.py
@@ -11,7 +11,9 @@
 ENTRIES, WTAB = 384, 32
 GROUPS = 3
 GF = FIELDS // GROUPS
+HALF = GF // 2
 SLABS = GF + 1
+CUT = HALF + 1
 AXES = ((0, 1, 2), (1, 2, 0), (2, 0, 1))
 F32, BF16, I32 = jnp.float32, jnp.bfloat16, jnp.int32
 
@@ -56,10 +58,9 @@
     dest_hbm,
     drow_hbm,
     wslot_hbm,
-    solved_hbm,
+    state,
     gain_ref,
     incoming_ref,
-    state,
     courant_ref,
     diff_ref,
     rate_ref,
@@ -80,7 +81,6 @@
     load_sem,
     entry_sem,
     small_sem,
-    store_sem,
     ag_send,
     ag_recv,
     halo_send,
@@ -145,11 +145,11 @@
         hot = (iota((CX, ENTRIES), 0) == spot).astype(F32).astype(BF16)
         kept = jnp.where((quarter == rel[q]) & (kind < 3), values, 0)
         table = lax.dot_general(kept.astype(F32).astype(BF16), hot, NT, preferred_element_type=F32)
-        gath[g, 0, 0, GF] = table.astype(BF16)
+        gath[g, 0, 0, 0] = table.astype(BF16)
 
     loads[0].wait()
     for g in range(GROUPS):
-        gath[g, 0, 0, :GF] = state[0, g * GF : (g + 1) * GF].astype(BF16)
+        gath[g, 0, 0, 1:] = state[0, g * GF : (g + 1) * GF].astype(BF16)
 
     pl.semaphore_wait(barrier, len(greeted))
 
@@ -163,16 +163,18 @@
             device_id_type=MESH,
         )
 
+    parts = (pl.ds(0, CUT), pl.ds(CUT, SLABS - CUT))
+
     def gather_copy(g, number):
         u, v = g, (g + 1) % 3
-        block = lambda i, j: gath.at[g, i, j]
         step = number % 3 + 1
         there = 4 - step
         others = pl.ds(1, 3)
         src, dst, axis = (
-            (block(0, 0), block(0, there), u),
-            (block(0, 0), block(there, 0), v),
-            (block(0, others), block(there, others), v),
+            (gath.at[g, 0, 0], gath.at[g, 0, there], u),
+            (gath.at[g, 0, 0, parts[0]], gath.at[g, there, 0, parts[0]], v),
+            (gath.at[g, 0, others, parts[0]], gath.at[g, there, others, parts[0]], v),
+            (gath.at[g, 0, :, parts[1]], gath.at[g, there, :, parts[1]], v),
         )[number // 3]
         return remote(
             src, dst, ag_send.at[g, number], ag_recv.at[g, number], (comp, shifted(axis, step))
@@ -266,6 +268,10 @@
             for n, value in enumerate(values):
                 strip_coef[side, k >> 2, k & 3, n] = value
 
+    for number in (9, 11, 10):
+        for g in range(GROUPS):
+            gather_copy(g, number).start()
+
     def strip_step(n, carry):
         half = n >> 2
         for j in range(4):
@@ -281,56 +287,63 @@
         i, r = p // 12, p % 12
         packed[p] = jnp.where(place < 4, roll_lanes(strips[1, i, r], -4), strips[0, i, r])
 
-    lax.fori_loop(12, 32, transport_step, 0)
+    lax.fori_loop(24, 32, transport_step, 0)
 
     small_loads[3].wait()
     rows_p, rows_q = iota((WTAB * CY, CX), 0), iota((256, CX), 0)
     lane_p = iota((1, CX), 1) >> 3
 
-    def scatter_copy(g, d):
+    def scatter_copy(part, g, d):
         target = (1 - comp, tile if d == 0 else shifted((g + 2) % 3, d))
         return remote(
-            outgoing.at[g, d], arrived.at[g, (4 - d) % 4], sc_send.at[g, d], sc_recv.at[g, d], target
+            outgoing.at[part, g, d],
+            arrived.at[part, g, (4 - d) % 4],
+            sc_send.at[part, g, d],
+            sc_recv.at[part, g, d],
+            target,
         )
 
-    def remap(g, carry):
-        for number in range(3, 9):
+    def remap(part, g, carry):
+        for number in range(3, 9) if part == 0 else range(9, 12):
             gather_copy(g, number).wait_recv()
-        table = jnp.zeros((CY, CX), F32)
-        for p in range(16):
-            rv, ru = p // 4, p % 4
-            offset = ((-ru % 4) * 4 + (-rv % 4)) * 8
-            moved = roll_lanes(gath[g, rv, ru, GF].astype(F32), p * 8 - offset)
-            table = jnp.where((lanes >> 3) == p, moved, table)
-        codes = table.astype(I32)
+        if part == 0:
+            table = jnp.zeros((CY, CX), F32)
+            for p in range(16):
+                rv, ru = p // 4, p % 4
+                offset = ((-ru % 4) * 4 + (-rv % 4)) * 8
+                moved = roll_lanes(gath[g, rv, ru, 0].astype(F32), p * 8 - offset)
+                table = jnp.where((lanes >> 3) == p, moved, table)
+            codes = table.astype(I32)
+            for d in range(4):
+                w_e, r_e, y_e = codes[d : d + 1], codes[4 + d : 5 + d], codes[8 + d : 9 + d]
+                into = (rows_p == jnp.where(y_e > 0, w_e * CY + y_e - 1, -1)).astype(F32).astype(BF16)
+                outof = (rows_q == lane_p * CY + r_e).astype(F32).astype(BF16)
+                pick[g, d] = lax.dot_general(into, outof, NT, preferred_element_type=F32).astype(BF16)
+        first = 1 + part * HALF
         for d in range(4):
-            w_e, r_e, y_e = codes[d : d + 1], codes[4 + d : 5 + d], codes[8 + d : 9 + d]
-            into = (rows_p == jnp.where(y_e > 0, w_e * CY + y_e - 1, -1)).astype(F32).astype(BF16)
-            outof = (rows_q == lane_p * CY + r_e).astype(F32).astype(BF16)
-            pick[d] = lax.dot_general(into, outof, NT, preferred_element_type=F32).astype(BF16)
-        for d in range(4):
-            for pair in range(GF // 2):
+            for pair in range(HALF // 2):
                 blocks = jnp.concatenate(
-                    [gath[g, :, :, 2 * pair + i].reshape(256, CX) for i in range(2)], axis=1
+                    [gath[g, :, :, first + 2 * pair + i].reshape(256, CX) for i in range(2)], axis=1
                 )
-                summed = jnp.dot(pick[d], blocks, preferred_element_type=F32).astype(BF16)
+                summed = jnp.dot(pick[g, d], blocks, preferred_element_type=F32).astype(BF16)
                 for i in range(2):
                     for w in range(WTAB):
-                        row = (d * GF + 2 * pair + i) * CY
+                        row = (d * HALF + 2 * pair + i) * CY
                         spread[w, row : row + CY] = summed[w * CY : (w + 1) * CY, i * CX : (i + 1) * CX]
-        transport_level(g)
+        transport_level(3 * part + g)
         table_all = jnp.concatenate([weight[w] for w in range(WTAB)], axis=1)
-        rows = GF * CY
+        rows = HALF * CY
         for d in range(0, 4, 2):
             chosen = jnp.concatenate([spread[w, d * rows : (d + 2) * rows] for w in range(WTAB)], axis=1)
             result = lax.dot_general(chosen, table_all, NT, preferred_element_type=F32).astype(BF16)
             for i in range(2):
-                outgoing[g, d + i] = result[i * rows : (i + 1) * rows].reshape(GF, CY, CX)
+                outgoing[part, g, d + i] = result[i * rows : (i + 1) * rows].reshape(HALF, CY, CX)
         for d in range(4):
-            scatter_copy(g, d).start()
-        return carry
-
-    lax.fori_loop(0, GROUPS, remap, 0)
+            scatter_copy(part, g, d).start()
+        return carry
+
+    for part in range(2):
+        lax.fori_loop(0, GROUPS, lambda g, carry, part=part: remap(part, g, carry), 0)
 
     small_loads[1].wait()
     small_loads[2].wait()
@@ -374,43 +387,28 @@
         return carry
 
     lax.fori_loop(0, FIELDS // 4, solve_fields, 0)
-    store = pltpu.make_async_copy(state, solved_hbm, store_sem)
-    store.start()
-
-    for g in range(GROUPS):
-        for d in range(4):
-            scatter_copy(g, d).wait_recv()
-        total = arrived[g, 0].astype(F32)
-        for d in range(1, 4):
-            total = total + arrived[g, d].astype(F32)
-        incoming_ref[g * GF : (g + 1) * GF] = total
+
+    for part in range(2):
+        for g in range(GROUPS):
+            for d in range(4):
+                scatter_copy(part, g, d).wait_recv()
+            total = arrived[part, g, 0].astype(F32)
+            for d in range(1, 4):
+                total = total + arrived[part, g, d].astype(F32)
+            start = (2 * g + part) * HALF
+            incoming_ref[start : start + HALF] = total
 
     def finish(g, carry):
-        for number in range(9):
+        for number in range(12):
             gather_copy(g, number).wait_send()
-        for d in range(4):
-            scatter_copy(g, d).wait_send()
+        for part in range(2):
+            for d in range(4):
+                scatter_copy(part, g, d).wait_send()
         return carry
 
     lax.fori_loop(0, GROUPS, finish, 0)
     for copy in halos:
         copy.wait_send()
-    store.wait()
-
-
-def combine(solved_hbm, gain_ref, incoming_ref, out_hbm, held, load_sem, store_sem):
-    loads = [pltpu.make_async_copy(solved_hbm.at[k], held.at[k], load_sem.at[k]) for k in range(LEV)]
-    stores = [pltpu.make_async_copy(held.at[k], out_hbm.at[k], store_sem.at[k]) for k in range(LEV)]
-    for load in loads:
-        load.start()
-    for k in range(LEV):
-        loads[k].wait()
-        gain = gain_ref[k]
-        for f in range(FIELDS):
-            held[k, f] = held[k, f] + gain * incoming_ref[f]
-        stores[k].start()
-    for store in stores:
-        store.wait()
 
 
 def per_device(
@@ -429,14 +427,13 @@
     solved, gain, incoming = pl.pallas_call(
         kernel,
         out_shape=(
-            jax.ShapeDtypeStruct((LEV, FIELDS) + plane, F32),
-            jax.ShapeDtypeStruct((LEV,) + plane, F32),
-            jax.ShapeDtypeStruct((FIELDS,) + plane, F32),
+            pltpu.VMEM((LEV, FIELDS) + plane, F32),
+            pltpu.VMEM((LEV,) + plane, F32),
+            pltpu.VMEM((FIELDS,) + plane, F32),
         ),
         in_specs=[hbm] * 9,
-        out_specs=(hbm, vmem, vmem),
+        out_specs=(vmem, vmem, vmem),
         scratch_shapes=[
-            pltpu.VMEM((LEV, FIELDS) + plane, F32),
             pltpu.VMEM((2, LEV) + plane, F32),
             pltpu.VMEM((LEV,) + plane, F32),
             pltpu.VMEM(plane, F32),
@@ -449,21 +446,20 @@
             pltpu.VMEM((2, 10) + plane, F32),
             pltpu.VMEM((LEV, 5) + plane, F32),
             pltpu.VMEM((GROUPS, 4, 4, SLABS) + plane, BF16),
-            pltpu.VMEM((4, WTAB * CY, 256), BF16),
-            pltpu.VMEM((WTAB, 4 * GF * CY, CX), BF16),
-            pltpu.VMEM((GROUPS, 4, GF) + plane, BF16),
-            pltpu.VMEM((GROUPS, 4, GF) + plane, BF16),
+            pltpu.VMEM((GROUPS, 4, WTAB * CY, 256), BF16),
+            pltpu.VMEM((WTAB, 4 * HALF * CY, CX), BF16),
+            pltpu.VMEM((2, GROUPS, 4, HALF) + plane, BF16),
+            pltpu.VMEM((2, GROUPS, 4, HALF) + plane, BF16),
             pltpu.VMEM((3, LEV) + plane, F32),
             pltpu.SemaphoreType.DMA((LEV,)),
             pltpu.SemaphoreType.DMA((4,)),
             pltpu.SemaphoreType.DMA((4,)),
-            pltpu.SemaphoreType.DMA,
-            pltpu.SemaphoreType.DMA((GROUPS, 9)),
-            pltpu.SemaphoreType.DMA((GROUPS, 9)),
+            pltpu.SemaphoreType.DMA((GROUPS, 12)),
+            pltpu.SemaphoreType.DMA((GROUPS, 12)),
             pltpu.SemaphoreType.DMA((2,)),
             pltpu.SemaphoreType.DMA((2,)),
-            pltpu.SemaphoreType.DMA((GROUPS, 4)),
-            pltpu.SemaphoreType.DMA((GROUPS, 4)),
+            pltpu.SemaphoreType.DMA((2, GROUPS, 4)),
+            pltpu.SemaphoreType.DMA((2, GROUPS, 4)),
         ],
         compiler_params=pltpu.CompilerParams(
             collective_id=0, has_side_effects=True, vmem_limit_bytes=60 * 2**20
@@ -480,20 +476,7 @@
         dest_row[0],
         weight_slot[0],
     )
-    out = pl.pallas_call(
-        combine,
-        out_shape=jax.ShapeDtypeStruct((LEV, FIELDS) + plane, F32),
-        in_specs=[hbm, vmem, vmem],
-        out_specs=hbm,
-        scratch_shapes=[
-            pltpu.VMEM((LEV, FIELDS) + plane, F32),
-            pltpu.SemaphoreType.DMA((LEV,)),
-            pltpu.SemaphoreType.DMA((LEV,)),
-        ],
-        compiler_params=pltpu.CompilerParams(vmem_limit_bytes=60 * 2**20),
-        name="combine",
-    )(solved, gain, incoming)
-    return out[None]
+    return (solved + gain[:, None] * incoming[None])[None]
 
 
 def solution(mesh):

time: 38.9 us -> 34.2 us (0.88)
  Pallas kernels: 38.7 us -> 32.7 us
  other arithmetic: 0 us -> 1.33 us
    pallas_call x2 -> x1, Pallas kernels: 38.7 us -> 32.7 us  [per_device(): pl.pallas_call(kernel, out_shape=(pltpu.VMEM((LEV, FIELDS) + plane, F32),...]
    broadcast_in_dim x0 -> x1, other arithmetic: none -> 1.33 us  [per_device(): return (solved + gain[:, None] * incoming[None])[None]]
where the time goes in v4:
time: 34.2 us; the launch traced here: 34 us
  Pallas kernels  32.7 us (96%)
  other arithmetic  1.33 us (4%)
    pallas_call x1, Pallas kernels, per_device(): pl.pallas_call(kernel, out_shape=(pltpu.VMEM((LEV, FIELDS) + plane, F32),...  32.7 us
    broadcast_in_dim x1, other arithmetic, per_device(): return (solved + gain[:, None] * incoming[None])[None]  1.33 us

profile of v4, /device:TPU:1, one launch (start us, length us, event | category | flops | bytes accessed | tf_op | source)
XLA Modules:
  0.0 34.0 jit_solution(13544427220699722133)
XLA Ops:
  0.0 32.7 %interval.1 = (f32[8,24,16,128]{3,2,1,0:T(8,128)S(1)}, f32[8,16,128]{2,1,0:T(8,128)S(1)}, f32[24,16,128]{2,1,0:T(8,128)S(1)}) custom-call(f32[8,24,16,128]{3,2,1,0:T(8,128)} %bitcast.10, f32[2,8,16,128]{3,2,1,0:T(8,128)} %bitcast.11, f32[8,16,128]{2,1,0:T(8,128)} %bitcast.12, f32[16,128]{1,0:T(8,128)} %bitcast.13, bf16[32,128,128]{2,1,0:T(8,128)(2,1)} %weight_hbm.1, ...), custom_call_target="tpu_custom_call" | custom-call | tf_op jit(solution)/shard_map/interval/pallas_call | solution.py:427
  32.7 1.3 %add_bitcast_fusion = f32[1,8,24,16,128]{4,3,2,1,0:T(8,128)} fusion(f32[8,24,16,128]{3,2,1,0:T(8,128)S(1)} %get-tuple-element.8, f32[24,16,128]{2,1,0:T(8,128)S(1)} %get-tuple-element.10, f32[8,16,128]{2,1,0:T(8,128)S(1)} %get-tuple-element.9), kind=kLoop, calls=%fused_computation | loop fusion | flops 786432 | bytes 3407872 | tf_op jit(solution)/shard_map/broadcast_in_dim | solution.py:479

commit v5 on v4

--- a/solution.py
+++ b/solution.py
@@ -287,8 +287,6 @@
         i, r = p // 12, p % 12
         packed[p] = jnp.where(place < 4, roll_lanes(strips[1, i, r], -4), strips[0, i, r])
 
-    lax.fori_loop(24, 32, transport_step, 0)
-
     small_loads[3].wait()
     rows_p, rows_q = iota((WTAB * CY, CX), 0), iota((256, CX), 0)
     lane_p = iota((1, CX), 1) >> 3
@@ -344,6 +342,7 @@
 
     for part in range(2):
         lax.fori_loop(0, GROUPS, lambda g, carry, part=part: remap(part, g, carry), 0)
+    lax.fori_loop(24, 32, transport_step, 0)
 
     small_loads[1].wait()
     small_loads[2].wait()

time: 34.2 us -> 33.1 us (0.968)
  Pallas kernels: 32.7 us -> 31.6 us
    pallas_call x1, Pallas kernels: 32.7 us -> 31.6 us  [per_device(): pl.pallas_call(kernel, out_shape=(pltpu.VMEM((LEV, FIELDS) + plane, F32),...]
where the time goes in v5:
time: 33.1 us; the launch traced here: 32.9 us
  Pallas kernels  31.6 us (95%)
  other arithmetic  1.33 us (4%)
    pallas_call x1, Pallas kernels, per_device(): pl.pallas_call(kernel, out_shape=(pltpu.VMEM((LEV, FIELDS) + plane, F32),...  31.6 us
    broadcast_in_dim x1, other arithmetic, per_device(): return (solved + gain[:, None] * incoming[None])[None]  1.33 us

profile of v5, /device:TPU:1, one launch (start us, length us, event | category | flops | bytes accessed | tf_op | source)
XLA Modules:
  0.0 32.9 jit_solution(574980864677159336)
XLA Ops:
  0.0 31.6 %interval.1 = (f32[8,24,16,128]{3,2,1,0:T(8,128)S(1)}, f32[8,16,128]{2,1,0:T(8,128)S(1)}, f32[24,16,128]{2,1,0:T(8,128)S(1)}) custom-call(f32[8,24,16,128]{3,2,1,0:T(8,128)} %bitcast.10, f32[2,8,16,128]{3,2,1,0:T(8,128)} %bitcast.11, f32[8,16,128]{2,1,0:T(8,128)} %bitcast.12, f32[16,128]{1,0:T(8,128)} %bitcast.13, bf16[32,128,128]{2,1,0:T(8,128)(2,1)} %weight_hbm.1, ...), custom_call_target="tpu_custom_call" | custom-call | tf_op jit(solution)/shard_map/interval/pallas_call | solution.py:426
  31.6 1.3 %add_bitcast_fusion = f32[1,8,24,16,128]{4,3,2,1,0:T(8,128)} fusion(f32[8,24,16,128]{3,2,1,0:T(8,128)S(1)} %get-tuple-element.8, f32[24,16,128]{2,1,0:T(8,128)S(1)} %get-tuple-element.10, f32[8,16,128]{2,1,0:T(8,128)S(1)} %get-tuple-element.9), kind=kLoop, calls=%fused_computation | loop fusion | flops 786432 | bytes 3407872 | tf_op jit(solution)/shard_map/broadcast_in_dim | solution.py:478

commit v6 on v5

--- a/solution.py
+++ b/solution.py
@@ -287,6 +287,27 @@
         i, r = p // 12, p % 12
         packed[p] = jnp.where(place < 4, roll_lanes(strips[1, i, r], -4), strips[0, i, r])
 
+    small_loads[1].wait()
+    small_loads[2].wait()
+    ratio = jnp.zeros((CY, CX), F32)
+    gain = None
+    gains, ratios = [], []
+    for k in range(LEV):
+        above = diff_ref[k] if k < LEV - 1 else jnp.zeros((CY, CX), F32)
+        below = diff_ref[k - 1] if k > 0 else jnp.zeros((CY, CX), F32)
+        inverse = 1.0 / (1.0 + below + above - below * ratio)
+        ratio = above * inverse
+        solve_coef[0, k] = inverse
+        solve_coef[1, k] = below * inverse
+        solve_coef[2, k] = ratio
+        gain = inverse if k == 0 else below * inverse * gain
+        gains.append(gain)
+        ratios.append(ratio)
+    value = jnp.zeros((CY, CX), F32)
+    for k in reversed(range(LEV)):
+        value = gains[k] + ratios[k] * value
+        gain_ref[k] = value * rate_ref[...]
+
     small_loads[3].wait()
     rows_p, rows_q = iota((WTAB * CY, CX), 0), iota((256, CX), 0)
     lane_p = iota((1, CX), 1) >> 3
@@ -336,34 +357,13 @@
             result = lax.dot_general(chosen, table_all, NT, preferred_element_type=F32).astype(BF16)
             for i in range(2):
                 outgoing[part, g, d + i] = result[i * rows : (i + 1) * rows].reshape(HALF, CY, CX)
-        for d in range(4):
+        for d in (2, 1, 3, 0):
             scatter_copy(part, g, d).start()
         return carry
 
     for part in range(2):
         lax.fori_loop(0, GROUPS, lambda g, carry, part=part: remap(part, g, carry), 0)
     lax.fori_loop(24, 32, transport_step, 0)
-
-    small_loads[1].wait()
-    small_loads[2].wait()
-    ratio = jnp.zeros((CY, CX), F32)
-    gain = None
-    gains, ratios = [], []
-    for k in range(LEV):
-        above = diff_ref[k] if k < LEV - 1 else jnp.zeros((CY, CX), F32)
-        below = diff_ref[k - 1] if k > 0 else jnp.zeros((CY, CX), F32)
-        inverse = 1.0 / (1.0 + below + above - below * ratio)
-        ratio = above * inverse
-        solve_coef[0, k] = inverse
-        solve_coef[1, k] = below * inverse
-        solve_coef[2, k] = ratio
-        gain = inverse if k == 0 else below * inverse * gain
-        gains.append(gain)
-        ratios.append(ratio)
-    value = jnp.zeros((CY, CX), F32)
-    for k in reversed(range(LEV)):
-        value = gains[k] + ratios[k] * value
-        gain_ref[k] = value * rate_ref[...]
 
     edge = (lanes < 4) | (lanes >= CX - 4)
 

time: 33.1 us -> 33 us (level)
  no operation moved by 1% of the time
where the time goes in v6:
time: 33 us; the launch traced here: 32.9 us
  Pallas kernels  31.5 us (95%)
  other arithmetic  1.33 us (4%)
    pallas_call x1, Pallas kernels, per_device(): pl.pallas_call(kernel, out_shape=(pltpu.VMEM((LEV, FIELDS) + plane, F32),...  31.5 us
    broadcast_in_dim x1, other arithmetic, per_device(): return (solved + gain[:, None] * incoming[None])[None]  1.33 us

profile of v6, /device:TPU:1, one launch (start us, length us, event | category | flops | bytes accessed | tf_op | source)
XLA Modules:
  0.0 32.9 jit_solution(8352257246514773058)
XLA Ops:
  0.0 31.5 %interval.1 = (f32[8,24,16,128]{3,2,1,0:T(8,128)S(1)}, f32[8,16,128]{2,1,0:T(8,128)S(1)}, f32[24,16,128]{2,1,0:T(8,128)S(1)}) custom-call(f32[8,24,16,128]{3,2,1,0:T(8,128)} %bitcast.10, f32[2,8,16,128]{3,2,1,0:T(8,128)} %bitcast.11, f32[8,16,128]{2,1,0:T(8,128)} %bitcast.12, f32[16,128]{1,0:T(8,128)} %bitcast.13, bf16[32,128,128]{2,1,0:T(8,128)(2,1)} %weight_hbm.1, ...), custom_call_target="tpu_custom_call" | custom-call | tf_op jit(solution)/shard_map/interval/pallas_call | solution.py:426
  31.5 1.3 %add_bitcast_fusion = f32[1,8,24,16,128]{4,3,2,1,0:T(8,128)} fusion(f32[8,24,16,128]{3,2,1,0:T(8,128)S(1)} %get-tuple-element.8, f32[24,16,128]{2,1,0:T(8,128)S(1)} %get-tuple-element.10, f32[8,16,128]{2,1,0:T(8,128)S(1)} %get-tuple-element.9), kind=kLoop, calls=%fused_computation | loop fusion | flops 786432 | bytes 3407872 | tf_op jit(solution)/shard_map/broadcast_in_dim | solution.py:478
